TPU v7x, 32 devices: a whole 2x2x4 slice. The times are simulated.
32 devices in a mesh: dp: 8 (over z, x), blk: 4 (over y, core).
Axes of the slice: x: 2, y: 2, z: 4, core: 2. Of those that a mesh axis runs over, the one named last changes fastest.
Arguments:
- embeddings: bfloat16 [8192, 768], P(('dp', 'blk')), may hold values from -6 to 6
- point_group: int32 [8192, 1], P(('dp', 'blk')), may hold values from 0 to 7; in each aligned block of 256 rows (0 to 255, 256 to 511, ...) at most 64 rows name the same one
- point_cluster: int32 [8192], P(('dp', 'blk')), may hold values from 0 to 31
- point_order: int32 [8192], P(('dp', 'blk')), may hold values from 0 to 8191, each once
Outputs:
- nearest: float32 [8192], P(('dp', 'blk'))
Inputs may be any that keep to these rules, and one draw needn't show every extreme that they name: `point_group`: among the rows of one device at most 64 name the same group, a bound that some blocks reach. `point_order`: every value appears once.
All inputs are finite; a program needn't handle non-finite values.
Results may differ from a plain program's by a relative error of at most 0.00077.
Values may be sent and summed in bfloat16 or wider, within the bound.
A program may use at most 64 MiB of HBM per device.

v0:
```python
import jax
import jax.numpy as jnp
from jax import lax
from jax.sharding import PartitionSpec as P

CLG = 32


def normalize(embeddings):
    values = embeddings.astype(jnp.float32)
    scale = lax.rsqrt(jnp.mean(values * values, axis=1, keepdims=True) + 1e-06)
    width = embeddings.shape[1]
    return (values * scale * width ** (-0.5)).astype(jnp.bfloat16)


def strongest(current, query, keys):
    query_rows, query_labels, query_order = query
    key_rows, key_labels, key_order = keys
    count = key_rows.shape[0]
    step = 512
    tiles = (
        key_rows.reshape(count // step, step, key_rows.shape[1]),
        key_labels.reshape(count // step, step),
        key_order.reshape(count // step, step),
    )

    def visit(best, block):
        rows, labels, order = block
        scores = lax.dot_general(
            query_rows, rows, (((1,), (1,)), ((), ())), preferred_element_type=jnp.float32
        )
        mask = (query_labels[:, None] == labels[None, :]) & (order[None, :] < query_order[:, None])
        return (jnp.maximum(best, jnp.max(jnp.where(mask, scores, -2.0), axis=1)), None)

    best, unused = lax.scan(visit, current, tiles)
    return best


def body(embeddings, point_group, point_cluster, point_order):
    groups = lax.axis_size("dp")
    blocks = lax.axis_size("blk")
    points = embeddings.shape[0]
    width = embeddings.shape[1]
    capacity = 2 * points // groups
    slots = groups * capacity
    unit = normalize(embeddings)
    group = point_group[:, 0]
    labels = group * CLG + point_cluster
    onehot = (group[:, None] == jnp.arange(groups, dtype=jnp.int32)[None, :]).astype(jnp.int32)
    before = jnp.cumsum(onehot, axis=0) - onehot
    target = group * capacity + jnp.sum(before * onehot, axis=1)
    send_rows = jnp.zeros((slots, width), jnp.bfloat16).at[target].set(unit)
    send_labels = jnp.full((slots,), -1, jnp.int32).at[target].set(labels)
    send_order = jnp.zeros((slots,), jnp.int32).at[target].set(point_order)
    floor_init = jnp.full((slots,), -2.0, jnp.float32)

    def widen(array):
        rest = array.shape[1:]
        sectioned = array.reshape((groups, 1, capacity) + rest)
        sectioned = jnp.broadcast_to(sectioned, (groups, blocks, capacity) + rest)
        return sectioned.reshape((groups * blocks * capacity,) + rest)

    arrived = (
        lax.all_to_all(widen(send_rows), ("dp", "blk"), split_axis=0, concat_axis=0, tiled=True),
        lax.all_to_all(widen(send_labels), ("dp", "blk"), split_axis=0, concat_axis=0, tiled=True),
        lax.all_to_all(widen(send_order), ("dp", "blk"), split_axis=0, concat_axis=0, tiled=True),
    )
    own_block = lax.axis_index("blk")

    def pick(array):
        rest = array.shape[1:]
        shaped = array.reshape((groups, blocks, capacity) + rest)
        return lax.dynamic_index_in_dim(shaped, own_block, 1, keepdims=False).reshape(
            (slots,) + rest
        )

    query = (pick(arrived[0]), pick(arrived[1]), pick(arrived[2]))
    best = strongest(floor_init, query, arrived)
    answer = jnp.where(best > -1.5, best, -1.0)
    returned = lax.all_to_all(answer, "dp", split_axis=0, concat_axis=0, tiled=True)
    return returned[target]


def solution(mesh):
    in_specs = (P(("dp", "blk"), None), P(("dp", "blk"), None), P(("dp", "blk")), P(("dp", "blk")))
    out_specs = P(("dp", "blk"))
    return jax.shard_map(body, mesh=mesh, in_specs=in_specs, out_specs=out_specs, check_vma=False)
```

profile of v0, /device:TPU:0, one launch (start us, length us, event | category | flops | bytes accessed | tf_op | source)
XLA Modules:
  0.0 129.6 jit_solution(172794172347789464)
XLA Ops:
  0.0 0.7 fusion.15
  0.7 0.6 reduce-window.6
  1.3 0.2 slice_reduce_fusion
  1.5 0.8 fusion.14
  2.3 0.7 compare_select_fusion
  3.0 0.7 multiply_add_fusion
  3.7 1.4 %scatter_custom_fusion = s32[512]{0:T(512)S(1)} fusion(s32[256]{0:T(256)S(1)} %bitcast.69, s32[256]{0:T(256)S(1)} %multiply_add_fusion, s32[]{:T(128)} %constant.56.clone.1), kind=kCustom, calls=%fused_computation.36 | custom fusion | bytes 2052 | tf_op jit(solution)/shard_map/scatter | solution.py:53
  5.1 0.1 broadcast_in_dim.51
  5.1 0.6 broadcast_in_dim.52
  5.7 7.3 %all-to-all-start = ((s32[32,64,1]{1,2,0:T(1,128)}), s32[32,64,1]{1,2,0:T(1,128)S(1)}, u32[]{:S(2)}, u32[]{:S(2)}) async-start(s32[32,64,1]{1,2,0:T(1,128)} %bitcast.6), calls=%async_computation | async-start | bytes 32768 | tf_op jit(solution)/shard_map/all_to_all | solution.py:65
  13.0 1.2 fusion.5
  14.2 1.6 %scatter_custom_fusion.1 = s32[512]{0:T(512)S(1)} fusion(s32[256]{0:T(256)S(1)} %bitcast.70, s32[256]{0:T(256)} %param.9, s32[]{:T(128)} %constant.16.clone.1), kind=kCustom, calls=%fused_computation.33 | custom fusion | bytes 2560 | tf_op jit(solution)/shard_map/scatter | solution.py:54
  15.8 0.1 broadcast_in_dim.54
  15.8 4.4 %all-to-all-done = s32[32,64,1]{1,2,0:T(1,128)S(1)} async-done(((s32[32,64,1]{1,2,0:T(1,128)}), s32[32,64,1]{1,2,0:T(1,128)S(1)}, u32[]{:S(2)}, u32[]{:S(2)}) %all-to-all-start) | async-done | bytes 8224 | tf_op jit(solution)/shard_map/all_to_all | solution.py:65
  20.2 0.6 broadcast_in_dim.55
  20.8 2.6 %all-to-all-start.1 = ((s32[32,64,1]{1,2,0:T(1,128)}), s32[32,64,1]{1,2,0:T(1,128)S(1)}, u32[]{:S(2)}, u32[]{:S(2)}) async-start(s32[32,64,1]{1,2,0:T(1,128)} %bitcast.9), calls=%async_computation.1 | async-start | bytes 32768 | tf_op jit(solution)/shard_map/all_to_all | solution.py:66
  23.4 2.4 %scatter_custom_fusion.2 = bf16[512,768]{1,0:T(8,128)(2,1)S(1)} fusion(s32[256]{0:T(256)S(1)} %bitcast.71, bf16[256,768]{1,0:T(8,128)(2,1)} %param.6, f32[]{:T(128)} %constant.37.clone.1, f32[256]{0:T(256)S(1)} %add_rsqrt_fusion, bf16[]{:T(256)} %constant.27.clone.1), kind=kCustom, calls=%fused_computation.18 | custom fusion | flops 786432 | bytes 1180678 | tf_op jit(solution)/shard_map/scatter | solution.py:52
  25.8 4.7 %all-to-all-done.1 = s32[32,64,1]{1,2,0:T(1,128)S(1)} async-done(((s32[32,64,1]{1,2,0:T(1,128)}), s32[32,64,1]{1,2,0:T(1,128)S(1)}, u32[]{:S(2)}, u32[]{:S(2)}) %all-to-all-start.1) | async-done | bytes 8224 | tf_op jit(solution)/shard_map/all_to_all | solution.py:66
  30.5 2.0 %broadcast_in_dim.58 = bf16[8,4,64,768]{3,2,1,0:T(8,128)(2,1)} broadcast(bf16[8,64,768]{2,1,0:T(8,128)(2,1)S(1)} %bitcast.56), dimensions={0,2,3} | broadcast | bytes 3932160 | tf_op jit(solution)/shard_map/broadcast_in_dim | solution.py:60
  32.5 2.8 %all-to-all-start.2 = ((bf16[32,64,768]{2,1,0:T(8,128)(2,1)}), bf16[32,64,768]{2,1,0:T(8,128)(2,1)S(1)}, u32[]{:S(2)}, u32[]{:S(2)}) async-start(bf16[32,64,768]{2,1,0:T(8,128)(2,1)} %bitcast.13), calls=%async_computation.2 | async-start | bytes 6291456 | tf_op jit(solution)/shard_map/all_to_all | solution.py:64
  35.3 0.5 broadcast.62
  35.8 0.6 reduce.11
  36.4 0.1 reshape.77
  36.5 0.6 reduce.12
  37.1 0.1 reshape.78
  37.2 0.0 copy-start
  37.2 0.1 lt.46
  37.3 0.0 copy-start.1
  37.3 0.1 eq.72
  37.4 69.8 %all-to-all-done.2 = bf16[32,64,768]{2,1,0:T(8,128)(2,1)S(1)} async-done(((bf16[32,64,768]{2,1,0:T(8,128)(2,1)}), bf16[32,64,768]{2,1,0:T(8,128)(2,1)S(1)}, u32[]{:S(2)}, u32[]{:S(2)}) %all-to-all-start.2) | async-done | bytes 3145760 | tf_op jit(solution)/shard_map/all_to_all | solution.py:64
  107.1 0.9 constant_dynamic-slice_fusion.2
  108.1 0.0 copy-done
  108.1 0.0 copy-done.1
  108.1 7.3 %while.12 = (s32[]{:T(128)}, f32[512]{0:T(512)S(1)}, s32[8,64]{1,0:T(8,128)}, s32[4,512]{1,0:T(4,128)S(1)}, s32[4,512]{1,0:T(4,128)S(1)}, /*index=5*/s32[8,64]{1...) while((s32[]{:T(128)}, f32[512]{0:T(512)S(1)}, ...), condition=%wide.wide.region_9.10_spmd.clone, body=%wide.wide.region_7.9_spmd.clone.sunk | while | flops 403964416 | bytes 1597583 | solution.py:35
  108.1 1.8 %fusion.29 = f32[512]{0:T(512)S(1)} fusion(bf16[512,768]{1,0:T(8,128)(2,1)} %get-tuple-element.222, bf16[4,512,768]{2,1,0:T(8,128)(2,1)S(1)} %get-tuple-element.221, s32[]{:T(128)S(6)} %copy.10, s32[512]{0:T(512)S(1)} %get-tuple-element.223, s32[512]{0:T(512)S(1)} %get-tuple-element.224, s32[512]{0:T(512)S(1)} %bitcast.60, s32[512]{0:T(512)S(1)} %bitcast.61), kind=kOutput, calls=%fused_computation.6.clone.clone.1 | convolution fusion | flops 403963392 | bytes 1583108 | tf_op jit(solution)/shard_map/while/body/eval_jaxpr/dot_general | solution.py:29
  109.9 1.8 %fusion.29 = f32[512]{0:T(512)S(1)} fusion(bf16[512,768]{1,0:T(8,128)(2,1)} %get-tuple-element.222, bf16[4,512,768]{2,1,0:T(8,128)(2,1)S(1)} %get-tuple-element.221, s32[]{:T(128)S(6)} %copy.10, s32[512]{0:T(512)S(1)} %get-tuple-element.223, s32[512]{0:T(512)S(1)} %get-tuple-element.224, s32[512]{0:T(512)S(1)} %bitcast.60, s32[512]{0:T(512)S(1)} %bitcast.61), kind=kOutput, calls=%fused_computation.6.clone.clone.1 | convolution fusion | flops 403963392 | bytes 1583108 | tf_op jit(solution)/shard_map/while/body/eval_jaxpr/dot_general | solution.py:29
  111.8 1.8 %fusion.29 = f32[512]{0:T(512)S(1)} fusion(bf16[512,768]{1,0:T(8,128)(2,1)} %get-tuple-element.222, bf16[4,512,768]{2,1,0:T(8,128)(2,1)S(1)} %get-tuple-element.221, s32[]{:T(128)S(6)} %copy.10, s32[512]{0:T(512)S(1)} %get-tuple-element.223, s32[512]{0:T(512)S(1)} %get-tuple-element.224, s32[512]{0:T(512)S(1)} %bitcast.60, s32[512]{0:T(512)S(1)} %bitcast.61), kind=kOutput, calls=%fused_computation.6.clone.clone.1 | convolution fusion | flops 403963392 | bytes 1583108 | tf_op jit(solution)/shard_map/while/body/eval_jaxpr/dot_general | solution.py:29
  113.6 1.8 %fusion.29 = f32[512]{0:T(512)S(1)} fusion(bf16[512,768]{1,0:T(8,128)(2,1)} %get-tuple-element.222, bf16[4,512,768]{2,1,0:T(8,128)(2,1)S(1)} %get-tuple-element.221, s32[]{:T(128)S(6)} %copy.10, s32[512]{0:T(512)S(1)} %get-tuple-element.223, s32[512]{0:T(512)S(1)} %get-tuple-element.224, s32[512]{0:T(512)S(1)} %bitcast.60, s32[512]{0:T(512)S(1)} %bitcast.61), kind=kOutput, calls=%fused_computation.6.clone.clone.1 | convolution fusion | flops 403963392 | bytes 1583108 | tf_op jit(solution)/shard_map/while/body/eval_jaxpr/dot_general | solution.py:29
  115.4 0.7 all_to_all.32
  116.1 3.3 %all-to-all-start.3 = ((f32[8,64,1]{1,2,0:T(1,128)}), f32[8,64,1]{1,2,0:T(1,128)S(1)}, u32[]{:S(2)}, u32[]{:S(2)}) async-start(f32[8,64,1]{1,2,0:T(1,128)} %bitcast.17), calls=%async_computation.3 | async-start | bytes 8192 | tf_op jit(solution)/shard_map/all_to_all | solution.py:80
  119.5 6.4 %all-to-all-done.3 = f32[8,64,1]{1,2,0:T(1,128)S(1)} async-done(((f32[8,64,1]{1,2,0:T(1,128)}), f32[8,64,1]{1,2,0:T(1,128)S(1)}, u32[]{:S(2)}, u32[]{:S(2)}) %all-to-all-start.3) | async-done | bytes 2080 | tf_op jit(solution)/shard_map/all_to_all | solution.py:80
  125.8 0.5 broadcast.64
  126.4 0.7 reduce.13
  127.0 0.1 all_to_all.34
  127.1 2.5 %gather_fusion = f32[256]{0:T(256)} fusion(f32[512]{0:T(512)S(1)} %all_to_all.34, s32[1024]{0:T(1024)S(1)} %pad_clamp_fusion), kind=kCustom, calls=%fused_computation | custom fusion | bytes 3072 | tf_op jit(solution)/shard_map/gather | solution.py:81
  (16 shorter events, 0.2 us)
Async XLA Ops:
  5.7 14.4 %all-to-all-start = ((s32[32,64,1]{1,2,0:T(1,128)}), s32[32,64,1]{1,2,0:T(1,128)S(1)}, u32[]{:S(2)}, u32[]{:S(2)}) async-start(s32[32,64,1]{1,2,0:T(1,128)} %bitcast.6), calls=%async_computation | async-start | bytes 32768 | tf_op jit(solution)/shard_map/all_to_all | solution.py:65
  20.8 9.7 %all-to-all-start.1 = ((s32[32,64,1]{1,2,0:T(1,128)}), s32[32,64,1]{1,2,0:T(1,128)S(1)}, u32[]{:S(2)}, u32[]{:S(2)}) async-start(s32[32,64,1]{1,2,0:T(1,128)} %bitcast.9), calls=%async_computation.1 | async-start | bytes 32768 | tf_op jit(solution)/shard_map/all_to_all | solution.py:66
  32.5 74.6 %all-to-all-start.2 = ((bf16[32,64,768]{2,1,0:T(8,128)(2,1)}), bf16[32,64,768]{2,1,0:T(8,128)(2,1)S(1)}, u32[]{:S(2)}, u32[]{:S(2)}) async-start(bf16[32,64,768]{2,1,0:T(8,128)(2,1)} %bitcast.13), calls=%async_computation.2 | async-start | bytes 6291456 | tf_op jit(solution)/shard_map/all_to_all | solution.py:64
  37.2 70.9 %copy-start = (s32[8,1,64]{2,1,0:T(1,128)}, s32[8,1,64]{2,1,0:T(1,128)S(1)}, u32[]{:S(2)}) copy-start(s32[8,1,64]{2,1,0:T(1,128)S(1)} %constant_dynamic-slice_fusion.3) | copy-start | bytes 6148
  37.3 70.8 %copy-start.1 = (s32[8,1,64]{2,1,0:T(1,128)}, s32[8,1,64]{2,1,0:T(1,128)S(1)}, u32[]{:S(2)}) copy-start(s32[8,1,64]{2,1,0:T(1,128)S(1)} %constant_dynamic-slice_fusion.4) | copy-start | bytes 6148
  116.1 9.7 %all-to-all-start.3 = ((f32[8,64,1]{1,2,0:T(1,128)}), f32[8,64,1]{1,2,0:T(1,128)S(1)}, u32[]{:S(2)}, u32[]{:S(2)}) async-start(f32[8,64,1]{1,2,0:T(1,128)} %bitcast.17), calls=%async_computation.3 | async-start | bytes 8192 | tf_op jit(solution)/shard_map/all_to_all | solution.py:80
where the time goes:
time: 130 us
  waiting for transfers between devices  85.2 us (66%)
  starting transfers between devices  16 us (12%)
  local copies, waits for them, and re-layouts  12.1 us (9%)
  other arithmetic  8.93 us (7%)
  matrix products  7.14 us (5%)
    all_to_all x1, waiting for transfers between devices, body(): lax.all_to_all(widen(send_rows), ('dp', 'blk'), split_axis=0, concat_axis...  69.8 us
    all_to_all x1, starting transfers between devices, body(): lax.all_to_all(widen(send_labels), ('dp', 'blk'), split_axis=0, concat_ax...  7.3 us
    dot_general x4, matrix products, visit(): lax.dot_general(query_rows, rows, (((1,), (1,)), ((), ())), preferred_ele...  7.14 us
    all_to_all x1, waiting for transfers between devices, body(): lax.all_to_all(answer, 'dp', split_axis=0, concat_axis=0, tiled=True)  6.39 us
    all_to_all x1, waiting for transfers between devices, body(): lax.all_to_all(widen(send_order), ('dp', 'blk'), split_axis=0, concat_axi...  4.69 us
    all_to_all x1, waiting for transfers between devices, body(): lax.all_to_all(widen(send_labels), ('dp', 'blk'), split_axis=0, concat_ax...  4.36 us
    broadcast_in_dim x5, local copies, waits for them, and re-layouts, widen(): sectioned = jnp.broadcast_to(sectioned, (groups, blocks, capacity) + rest)  3.38 us
    all_to_all x1, starting transfers between devices, body(): lax.all_to_all(answer, 'dp', split_axis=0, concat_axis=0, tiled=True)  3.33 us
  transfers between devices with their start and end apart: 4, of which 4 were waited for; matrix products, arithmetic and copies ran while one was open for 6% of the time, Pallas kernels for 0%

commit v1 on v0

v1 whole, which is shorter than its diff:
```python
import functools

import jax
import jax.numpy as jnp
from jax import lax
from jax.experimental import pallas as pl
from jax.experimental.pallas import tpu as pltpu
from jax.sharding import PartitionSpec as P

CLG = 32
LANES = 128
MESH = pl.DeviceIdType.MESH
NT = (((1,), (1,)), ((), ()))


def flip(index, mask):
    out = index
    bit = 1
    while bit <= mask:
        if mask & bit:
            digit = lax.rem(lax.div(index, jnp.int32(bit)), jnp.int32(2))
            out = out + bit * (1 - 2 * digit)
        bit *= 2
    return out


def kernel(groups, total, order, emb_ref, ids_ref, out_ref, send, keys, msend, meta, kmeta, res, back,
           s1, r1, sm, rm, sy, ry, sc, rc, sd, rd, smx, rmx, sb, rb):
    points, width = emb_ref.shape
    cap = 2 * points // groups
    slots = groups * cap
    per = LANES // cap
    tiles = slots // LANES
    me = lax.axis_index("dp")
    own = lax.axis_index("blk")
    across = {"blk": flip(own, 2)}
    beside = {"blk": flip(own, 1)}
    partner = [None] + [{"dp": flip(me, k)} for k in range(1, groups)]

    barrier = pltpu.get_barrier_semaphore()
    for who in partner[1:] + [across, beside]:
        pl.semaphore_signal(barrier, inc=1, device_id=who, device_id_type=MESH)

    def remote(src, dst, ssem, rsem, who):
        return pltpu.make_async_remote_copy(
            src_ref=src, dst_ref=dst, send_sem=ssem, recv_sem=rsem, device_id=who, device_id_type=MESH
        )

    group = ids_ref[0:1, :]
    combined = ids_ref[1:2, :] * total + ids_ref[2:3, :] + 1
    relative = jnp.bitwise_xor(group, me)
    member = lax.broadcasted_iota(jnp.int32, (groups, points), 0) == relative
    member_f = jnp.where(member, 1.0, 0.0)
    earlier = lax.broadcasted_iota(jnp.int32, (points, points), 0) < lax.broadcasted_iota(
        jnp.int32, (points, points), 1
    )
    before = jnp.dot(
        member_f.astype(jnp.bfloat16),
        jnp.where(earlier, 1.0, 0.0).astype(jnp.bfloat16),
        preferred_element_type=jnp.float32,
    )
    rank = jnp.sum(before * member_f, axis=0, keepdims=True).astype(jnp.int32)
    target = relative * cap + rank

    digits = jnp.concatenate(
        [combined & 127, (combined >> 7) & 127, combined >> 14, jnp.zeros((5, points), jnp.int32)], axis=0
    ).astype(jnp.float32).astype(jnp.bfloat16)
    lane_slot = lax.broadcasted_iota(jnp.int32, (LANES, points), 0) & (cap - 1)
    local_target = target & (cap - 1)
    same_rank = lane_slot == local_target
    for k in range(groups):
        pick = jnp.where(same_rank & (relative == k), 1.0, 0.0).astype(jnp.bfloat16)
        got = lax.dot_general(digits, pick, NT, preferred_element_type=jnp.float32)
        row = got[0:1, :] + 128.0 * got[1:2, :] + 16384.0 * got[2:3, :]
        row = jnp.broadcast_to(row.astype(jnp.int32), (8, LANES))
        if k == 0:
            meta[0, 0] = row
        else:
            msend[k] = row

    values = emb_ref[...].astype(jnp.float32)
    scale = lax.rsqrt(jnp.mean(values * values, axis=1, keepdims=True) + 1e-06)
    unit = (values * scale * width ** (-0.5)).astype(jnp.bfloat16)

    pl.semaphore_wait(barrier, groups + 1)

    started = []
    meta_copies = [None] * groups
    for k in order:
        meta_copies[k] = remote(msend.at[k], meta.at[0, k], sm.at[k], rm.at[k], partner[k])
        meta_copies[k].start()

    first = [None] * groups
    over_y = [None] * groups
    over_c = [None] * groups
    diag = [None] * groups

    def forward(k):
        over_y[k] = remote(keys.at[0, k], keys.at[2, k], sy.at[k], ry.at[k], across)
        over_y[k].start()
        over_c[k] = remote(keys.at[0, k], keys.at[1, k], sc.at[k], rc.at[k], beside)
        over_c[k].start()

    def onward(k):
        over_y[k].wait_recv()
        diag[k] = remote(keys.at[2, k], keys.at[3, k], sd.at[k], rd.at[k], beside)
        diag[k].start()

    slot_rows = lax.broadcasted_iota(jnp.int32, (cap, points), 0)
    for k in [order[0], 0] + list(order[1:]):
        place = jnp.where(slot_rows + k * cap == target, 1.0, 0.0).astype(jnp.bfloat16)
        rows = jnp.dot(place, unit, preferred_element_type=jnp.float32).astype(jnp.bfloat16)
        if k == 0:
            keys[0, 0] = rows
            forward(0)
        else:
            send[k] = rows
            first[k] = remote(send.at[k], keys.at[0, k], s1.at[k], r1.at[k], partner[k])
            first[k].start()

    def key_tiles(r):
        lane_block = lax.broadcasted_iota(jnp.int32, (1, LANES), 1) // cap
        rows = []
        for t in range(tiles):
            row = meta[r, t * per][0:1, :]
            for j in range(1, per):
                row = jnp.where(lane_block == j, meta[r, t * per + j][0:1, :], row)
            rows.append(row)
            kmeta[r, t] = jnp.broadcast_to(row, (LANES, LANES)).T
        return rows

    for k in order:
        meta_copies[k].wait_recv()
    meta_y = remote(meta.at[0], meta.at[2], smx.at[0], rmx.at[0], across)
    meta_y.start()
    meta_c = remote(meta.at[0], meta.at[1], smx.at[1], rmx.at[1], beside)
    meta_c.start()
    query = jnp.concatenate(key_tiles(0), axis=1)
    floor = (query - 1) & (-total)

    arrive = sorted(order, key=lambda k: (k.bit_length(), k))
    queue = [0]
    for k in arrive:
        first[k].wait_recv()
        forward(k)
        onward(queue.pop(0))
        queue.append(k)
        if k == 1:
            meta_y.wait_recv()
            meta_d = remote(meta.at[2], meta.at[3], smx.at[2], rmx.at[2], beside)
            meta_d.start()
    meta_c.wait_recv()
    key_tiles(1)
    key_tiles(2)
    meta_d.wait_recv()
    key_tiles(3)

    queries = keys[0].reshape(slots, width)
    half = groups // 2

    def visit(best, r, h):
        block = keys[r, h * half:(h + 1) * half].reshape(half * cap, width)
        scores = lax.dot_general(block, queries, NT, preferred_element_type=jnp.float32)
        for t in range(tiles // 2):
            mine = kmeta[r, h * (tiles // 2) + t]
            mine = jnp.concatenate([mine] * tiles, axis=1)
            part = jnp.where((mine < query) & (mine > floor), scores[t * LANES:(t + 1) * LANES], -2.0)
            best = jnp.maximum(best, jnp.max(part.reshape(LANES // 8, 8, slots), axis=0))
        return best

    best = jnp.full((8, slots), -2.0, jnp.float32)
    best = visit(best, 0, 0)
    onward(queue.pop(0))
    for r in (0, 1, 2, 3):
        for h in (0, 1):
            if r == 0 and h == 0:
                continue
            if r == 1 or r == 3:
                for k in range(h * half, (h + 1) * half):
                    (over_c if r == 1 else diag)[k].wait_recv()
            best = visit(best, r, h)
    best = jnp.max(best, axis=0, keepdims=True)
    answer = jnp.broadcast_to(jnp.where(best > -1.5, best, -1.0), (8, slots))
    for t in range(tiles):
        res[t] = answer[:, t * LANES:(t + 1) * LANES]
    back[0] = res[0]
    replies = [None] * groups
    for k in order:
        replies[k] = remote(res.at[k // per], back.at[k], sb.at[k], rb.at[k], partner[k])
        replies[k].start()

    for k in range(groups):
        over_y[k].wait_send()
        over_c[k].wait_send()
        diag[k].wait_send()
        if k:
            first[k].wait_send()
            meta_copies[k].wait_send()
    meta_y.wait_send()
    meta_c.wait_send()
    meta_d.wait_send()

    lane_block = lax.broadcasted_iota(jnp.int32, (1, LANES), 1) // cap
    nearest = jnp.full((1, points), -2.0, jnp.float32)
    slot_iota = lax.broadcasted_iota(jnp.int32, (LANES, points), 0)
    for t in range(tiles):
        for j in range(per):
            if t * per + j:
                replies[t * per + j].wait_recv()
        row = back[t * per][0:1, :]
        for j in range(1, per):
            row = jnp.where(lane_block == j, back[t * per + j][0:1, :], row)
        column = jnp.broadcast_to(row, (LANES, LANES)).T
        column = jnp.concatenate([column] * (points // LANES), axis=1)
        hit = jnp.where(slot_iota + t * LANES == target, column, -2.0)
        nearest = jnp.maximum(nearest, jnp.max(hit, axis=0, keepdims=True))
    out_ref[...] = nearest
    for k in order:
        replies[k].wait_send()


def body(total, embeddings, point_group, point_cluster, point_order):
    groups = lax.axis_size("dp")
    blocks = lax.axis_size("blk")
    points, width = embeddings.shape
    cap = 2 * points // groups
    slots = groups * cap
    ids = jnp.stack([point_group[:, 0], point_cluster, point_order])
    order = [k for k in range(groups // 2, groups)] + [k for k in range(1, groups // 2)]
    dma = pltpu.SemaphoreType.DMA
    out = pl.pallas_call(
        functools.partial(kernel, groups, total, order),
        out_shape=jax.ShapeDtypeStruct((1, points), jnp.float32),
        in_specs=[pl.BlockSpec(memory_space=pltpu.VMEM)] * 2,
        out_specs=pl.BlockSpec(memory_space=pltpu.VMEM),
        scratch_shapes=[
            pltpu.VMEM((groups, cap, width), jnp.bfloat16),
            pltpu.VMEM((blocks, groups, cap, width), jnp.bfloat16),
            pltpu.VMEM((groups, 8, LANES), jnp.int32),
            pltpu.VMEM((blocks, groups, 8, LANES), jnp.int32),
            pltpu.VMEM((blocks, slots // LANES, LANES, LANES), jnp.int32),
            pltpu.VMEM((slots // LANES, 8, LANES), jnp.float32),
            pltpu.VMEM((groups, 8, LANES), jnp.float32),
        ]
        + [dma((groups,))] * 10
        + [dma((3,))] * 2
        + [dma((groups,))] * 2,
        compiler_params=pltpu.CompilerParams(
            collective_id=0, has_side_effects=True, vmem_limit_bytes=48 * 1024 * 1024
        ),
        cost_estimate=pl.CostEstimate(
            flops=2 * slots * slots * blocks * width, bytes_accessed=points * width * 2, transcendentals=points
        ),
    )(embeddings, ids)
    return out.reshape(points)


def solution(mesh):
    in_specs = (P(("dp", "blk"), None), P(("dp", "blk"), None), P(("dp", "blk")), P(("dp", "blk")))
    out_specs = P(("dp", "blk"))

    def run(embeddings, point_group, point_cluster, point_order):
        inner = functools.partial(body, embeddings.shape[0])
        return jax.shard_map(inner, mesh=mesh, in_specs=in_specs, out_specs=out_specs, check_vma=False)(
            embeddings, point_group, point_cluster, point_order
        )

    return run
```

time: 130 us -> 44 us (0.34)
  waiting for transfers between devices: 85.2 us -> 0 us
  Pallas kernels: 0 us -> 41.6 us
  starting transfers between devices: 16 us -> 0 us
  local copies, waits for them, and re-layouts: 12.1 us -> 2.26 us
  other arithmetic: 8.93 us -> 0.01 us
  matrix products: 7.14 us -> 0 us
    all_to_all x4 -> x0, waiting for transfers between devices: 85.2 us -> none  [the longest x1 69.8 us: body(): lax.all_to_all(widen(send_rows), ('dp', 'blk'), split_axis=0, concat_axis...]
    pallas_call x0 -> x1, Pallas kernels: none -> 41.6 us  [body(): pl.pallas_call(functools.partial(kernel, groups, total, order), out_shape...]
    all_to_all x4 -> x0, starting transfers between devices: 16 us -> none  [the longest x1 7.3 us: body(): lax.all_to_all(widen(send_labels), ('dp', 'blk'), split_axis=0, concat_ax...]
    dot_general x4 -> x0, matrix products: 7.14 us -> none  [visit(): lax.dot_general(query_rows, rows, (((1,), (1,)), ((), ())), preferred_ele...]
    broadcast_in_dim x5 -> x0, local copies, waits for them, and re-layouts: 3.38 us -> none  [widen(): sectioned = jnp.broadcast_to(sectioned, (groups, blocks, capacity) + rest)]
    scatter x2 -> x0, local copies, waits for them, and re-layouts: 2.95 us -> none  [the longest x1 1.55 us: body(): send_order = jnp.zeros((slots,), jnp.int32).at[target].set(point_order)]
    gather x1 -> x0, local copies, waits for them, and re-layouts: 2.5 us -> none  [body(): return returned[target]]
    scatter x1 -> x0, other arithmetic: 2.43 us -> none  [body(): send_rows = jnp.zeros((slots, width), jnp.bfloat16).at[target].set(unit)]
  transfers between devices with their start and end apart: 4 -> 0, of which waited for: 4 -> 0; matrix products, arithmetic and copies ran while one was open for 6% -> 0% of each run, Pallas kernels for 0% -> 0%
where the time goes in v1:
time: 44 us; the launch traced here: 43.8 us
  Pallas kernels  41.6 us (95%)
  local copies, waits for them, and re-layouts  2.26 us (5%)
    pallas_call x1, Pallas kernels, body(): pl.pallas_call(functools.partial(kernel, groups, total, order), out_shape...  41.6 us
    unnamed x9, local copies, waits for them, and re-layouts  2.26 us

profile of v1, /device:TPU:0, one launch (start us, length us, event | category | flops | bytes accessed | tf_op | source)
XLA Modules:
  0.0 43.8 jit_solution(7811259450550641019)
XLA Ops:
  0.0 0.0 copy-start.2
  0.0 0.0 copy-start.3
  0.0 0.0 copy-start.1
  0.0 0.7 %copy-done.2 = s32[256]{0:T(256)S(1)} copy-done((s32[256]{0:T(256)S(1)}, s32[256]{0:T(256)}, u32[]{:S(2)}) %copy-start.2) | copy-done | bytes 1048
  0.7 0.0 copy-done.3
  0.7 0.0 copy-done.1
  0.7 0.0 copy-start
  0.7 1.0 %copy-done = bf16[256,768]{1,0:T(8,128)(2,1)S(1)} copy-done((bf16[256,768]{1,0:T(8,128)(2,1)S(1)}, bf16[256,768]{1,0:T(8,128)(2,1)}, u32[]{:S(2)}) %copy-start) | copy-done | bytes 393240
  1.7 41.6 %shard_map.46 = f32[1,256]{1,0:T(1,128)S(1)} custom-call(bf16[256,768]{1,0:T(8,128)(2,1)S(1)} %copy-done, s32[3,256]{1,0:T(4,128)S(1)} %pad_add_fusion.ids_ref), custom_call_target="tpu_custom_call" | custom-call | flops 1610612736 | bytes 393216 | tf_op jit(solution)/shard_map/pallas_call | solution.py:231
  43.3 0.6 %copy.6 = f32[256]{0:T(256)} copy(f32[256]{0:T(256)S(1)} %bitcast.4) | data formatting | bytes 2048
  (1 shorter events, 0.0 us)
Async XLA Ops:
  0.0 0.7 %copy-start.2 = (s32[256]{0:T(256)S(1)}, s32[256]{0:T(256)}, u32[]{:S(2)}) copy-start(s32[256]{0:T(256)} %param.6) | copy-start | bytes 3076
  0.0 0.7 %copy-start.3 = (s32[256,1]{0,1:T(1,128)S(1)}, s32[256,1]{0,1:T(1,128)}, u32[]{:S(2)}) copy-start(s32[256,1]{0,1:T(1,128)} %param.5) | copy-start | bytes 3076
  0.0 0.7 %copy-start.1 = (s32[256]{0:T(256)S(1)}, s32[256]{0:T(256)}, u32[]{:S(2)}) copy-start(s32[256]{0:T(256)} %param.7) | copy-start | bytes 3076
  0.7 1.0 %copy-start = (bf16[256,768]{1,0:T(8,128)(2,1)S(1)}, bf16[256,768]{1,0:T(8,128)(2,1)}, u32[]{:S(2)}) copy-start(bf16[256,768]{1,0:T(8,128)(2,1)} %emb_ref.1) | copy-start | bytes 1179652

commit v2 on v1

--- a/solution.py
+++ b/solution.py
@@ -24,8 +24,8 @@
     return out
 
 
-def kernel(groups, total, order, emb_ref, ids_ref, out_ref, send, keys, msend, meta, kmeta, res, back,
-           s1, r1, sm, rm, sy, ry, sc, rc, sd, rd, smx, rmx, sb, rb):
+def kernel(groups, total, order, emb_hbm, group_hbm, cluster_hbm, order_hbm, out_ref, emb_ref, ids, fetched,
+           send, keys, msend, meta, kmeta, res, back, s1, r1, sm, rm, sy, ry, sc, rc, sd, rd, smx, rmx, sb, rb):
     points, width = emb_ref.shape
     cap = 2 * points // groups
     slots = groups * cap
@@ -37,6 +37,15 @@
     beside = {"blk": flip(own, 1)}
     partner = [None] + [{"dp": flip(me, k)} for k in range(1, groups)]
 
+    fetches = [
+        pltpu.make_async_copy(group_hbm, ids.at[0], fetched.at[0]),
+        pltpu.make_async_copy(cluster_hbm, ids.at[1], fetched.at[1]),
+        pltpu.make_async_copy(order_hbm, ids.at[2], fetched.at[2]),
+        pltpu.make_async_copy(emb_hbm, emb_ref, fetched.at[3]),
+    ]
+    for fetch in fetches:
+        fetch.start()
+
     barrier = pltpu.get_barrier_semaphore()
     for who in partner[1:] + [across, beside]:
         pl.semaphore_signal(barrier, inc=1, device_id=who, device_id_type=MESH)
@@ -46,8 +55,10 @@
             src_ref=src, dst_ref=dst, send_sem=ssem, recv_sem=rsem, device_id=who, device_id_type=MESH
         )
 
-    group = ids_ref[0:1, :]
-    combined = ids_ref[1:2, :] * total + ids_ref[2:3, :] + 1
+    for fetch in fetches[:3]:
+        fetch.wait()
+    group = ids[0]
+    combined = ids[1] * total + ids[2] + 1
     relative = jnp.bitwise_xor(group, me)
     member = lax.broadcasted_iota(jnp.int32, (groups, points), 0) == relative
     member_f = jnp.where(member, 1.0, 0.0)
@@ -78,6 +89,7 @@
         else:
             msend[k] = row
 
+    fetches[3].wait()
     values = emb_ref[...].astype(jnp.float32)
     scale = lax.rsqrt(jnp.mean(values * values, axis=1, keepdims=True) + 1e-06)
     unit = (values * scale * width ** (-0.5)).astype(jnp.bfloat16)
@@ -138,14 +150,13 @@
     query = jnp.concatenate(key_tiles(0), axis=1)
     floor = (query - 1) & (-total)
 
-    arrive = sorted(order, key=lambda k: (k.bit_length(), k))
     queue = [0]
-    for k in arrive:
+    for k in order:
         first[k].wait_recv()
         forward(k)
         onward(queue.pop(0))
         queue.append(k)
-        if k == 1:
+        if k == order[1]:
             meta_y.wait_recv()
             meta_d = remote(meta.at[2], meta.at[3], smx.at[2], rmx.at[2], beside)
             meta_d.start()
@@ -225,15 +236,18 @@
     points, width = embeddings.shape
     cap = 2 * points // groups
     slots = groups * cap
-    ids = jnp.stack([point_group[:, 0], point_cluster, point_order])
-    order = [k for k in range(groups // 2, groups)] + [k for k in range(1, groups // 2)]
+    near, far = list(range(1, groups // 2)), list(range(groups // 2, groups))
+    order = [k for pair in zip(near, far) for k in pair] + far[len(near):]
     dma = pltpu.SemaphoreType.DMA
     out = pl.pallas_call(
         functools.partial(kernel, groups, total, order),
         out_shape=jax.ShapeDtypeStruct((1, points), jnp.float32),
-        in_specs=[pl.BlockSpec(memory_space=pltpu.VMEM)] * 2,
+        in_specs=[pl.BlockSpec(memory_space=pl.ANY)] * 4,
         out_specs=pl.BlockSpec(memory_space=pltpu.VMEM),
         scratch_shapes=[
+            pltpu.VMEM((points, width), jnp.bfloat16),
+            pltpu.VMEM((3, 1, points), jnp.int32),
+            dma((4,)),
             pltpu.VMEM((groups, cap, width), jnp.bfloat16),
             pltpu.VMEM((blocks, groups, cap, width), jnp.bfloat16),
             pltpu.VMEM((groups, 8, LANES), jnp.int32),
@@ -246,12 +260,12 @@
         + [dma((3,))] * 2
         + [dma((groups,))] * 2,
         compiler_params=pltpu.CompilerParams(
-            collective_id=0, has_side_effects=True, vmem_limit_bytes=48 * 1024 * 1024
+            collective_id=0, has_side_effects=True, vmem_limit_bytes=64 * 1024 * 1024 - 65536
         ),
         cost_estimate=pl.CostEstimate(
             flops=2 * slots * slots * blocks * width, bytes_accessed=points * width * 2, transcendentals=points
         ),
-    )(embeddings, ids)
+    )(embeddings, point_group.reshape(1, points), point_cluster.reshape(1, points), point_order.reshape(1, points))
     return out.reshape(points)
 
 

time: 44 us -> 40.2 us (0.914)
  Pallas kernels: 41.6 us -> 38.9 us
  local copies, waits for them, and re-layouts: 2.26 us -> 1.22 us
    pallas_call x1, Pallas kernels: 41.6 us -> 38.9 us  [body(): pl.pallas_call(functools.partial(kernel, groups, total, order), out_shape...]
    unnamed x9 -> x3, local copies, waits for them, and re-layouts: 2.26 us -> 1.22 us
where the time goes in v2:
time: 40.2 us; the launch traced here: 40.1 us
  Pallas kernels  38.9 us (97%)
  local copies, waits for them, and re-layouts  1.22 us (3%)
    pallas_call x1, Pallas kernels, body(): pl.pallas_call(functools.partial(kernel, groups, total, order), out_shape...  38.9 us
    unnamed x3, local copies, waits for them, and re-layouts  1.22 us

profile of v2, /device:TPU:0, one launch (start us, length us, event | category | flops | bytes accessed | tf_op | source)
XLA Modules:
  0.0 40.1 jit_solution(7840655867805594926)
XLA Ops:
  0.0 38.9 %shard_map.46 = f32[1,256]{1,0:T(1,128)} custom-call(bf16[256,768]{1,0:T(8,128)(2,1)} %emb_hbm.1, s32[1,256]{1,0:T(1,128)} %bitcast.5, s32[1,256]{1,0:T(1,128)} %bitcast.6, s32[1,256]{1,0:T(1,128)} %bitcast.7), custom_call_target="tpu_custom_call" | custom-call | flops 1610612736 | bytes 393216 | tf_op jit(solution)/shard_map/pallas_call | solution.py:242
  38.9 0.0 copy-start
  38.9 0.7 %copy-done = f32[1,256]{1,0:T(1,128)S(1)} copy-done((f32[1,256]{1,0:T(1,128)S(1)}, f32[1,256]{1,0:T(1,128)}, u32[]{:S(2)}) %copy-start) | copy-done | bytes 1048
  39.5 0.6 %copy.6 = f32[256]{0:T(256)} copy(f32[256]{0:T(256)S(1)} %bitcast.4) | data formatting | bytes 2048
Async XLA Ops:
  38.9 0.7 %copy-start = (f32[1,256]{1,0:T(1,128)S(1)}, f32[1,256]{1,0:T(1,128)}, u32[]{:S(2)}) copy-start(f32[1,256]{1,0:T(1,128)} %shard_map.46) | copy-start | bytes 3076

commit v3 on v2

--- a/solution.py
+++ b/solution.py
@@ -119,6 +119,8 @@
         diag[k].start()
 
     slot_rows = lax.broadcasted_iota(jnp.int32, (cap, points), 0)
+    window = groups // 4
+    held_back = [k for k in order if k >= groups // 2][window:]
     for k in [order[0], 0] + list(order[1:]):
         place = jnp.where(slot_rows + k * cap == target, 1.0, 0.0).astype(jnp.bfloat16)
         rows = jnp.dot(place, unit, preferred_element_type=jnp.float32).astype(jnp.bfloat16)
@@ -128,7 +130,8 @@
         else:
             send[k] = rows
             first[k] = remote(send.at[k], keys.at[0, k], s1.at[k], r1.at[k], partner[k])
-            first[k].start()
+            if k not in held_back:
+                first[k].start()
 
     def key_tiles(r):
         lane_block = lax.broadcasted_iota(jnp.int32, (1, LANES), 1) // cap
@@ -153,6 +156,8 @@
     queue = [0]
     for k in order:
         first[k].wait_recv()
+        if k >= groups // 2 and held_back:
+            first[held_back.pop(0)].start()
         forward(k)
         onward(queue.pop(0))
         queue.append(k)
@@ -225,7 +230,7 @@
         column = jnp.concatenate([column] * (points // LANES), axis=1)
         hit = jnp.where(slot_iota + t * LANES == target, column, -2.0)
         nearest = jnp.maximum(nearest, jnp.max(hit, axis=0, keepdims=True))
-    out_ref[...] = nearest
+    out_ref[...] = nearest.reshape(points)
     for k in order:
         replies[k].wait_send()
 
@@ -241,7 +246,7 @@
     dma = pltpu.SemaphoreType.DMA
     out = pl.pallas_call(
         functools.partial(kernel, groups, total, order),
-        out_shape=jax.ShapeDtypeStruct((1, points), jnp.float32),
+        out_shape=jax.ShapeDtypeStruct((points,), jnp.float32),
         in_specs=[pl.BlockSpec(memory_space=pl.ANY)] * 4,
         out_specs=pl.BlockSpec(memory_space=pltpu.VMEM),
         scratch_shapes=[
@@ -266,7 +271,7 @@
             flops=2 * slots * slots * blocks * width, bytes_accessed=points * width * 2, transcendentals=points
         ),
     )(embeddings, point_group.reshape(1, points), point_cluster.reshape(1, points), point_order.reshape(1, points))
-    return out.reshape(points)
+    return out
 
 
 def solution(mesh):

time: 40.2 us -> 40 us (level)
    unnamed x3 -> x1, local copies, waits for them, and re-layouts: 1.22 us -> 1.24 us
where the time goes in v3:
time: 40 us; the launch traced here: 39.9 us
  Pallas kernels  38.6 us (96%)
  local copies, waits for them, and re-layouts  1.24 us (3%)
    pallas_call x1, Pallas kernels, body(): pl.pallas_call(functools.partial(kernel, groups, total, order), out_shape...  38.6 us
    unnamed x1, local copies, waits for them, and re-layouts  1.24 us

profile of v3, /device:TPU:0, one launch (start us, length us, event | category | flops | bytes accessed | tf_op | source)
XLA Modules:
  0.0 39.9 jit_solution(13262333423131346313)
XLA Ops:
  0.0 38.6 %shard_map.46 = f32[256]{0:T(256)} custom-call(bf16[256,768]{1,0:T(8,128)(2,1)} %emb_hbm.1, s32[1,256]{1,0:T(1,128)} %bitcast.3, s32[1,256]{1,0:T(1,128)} %bitcast.4, s32[1,256]{1,0:T(1,128)} %bitcast.5), custom_call_target="tpu_custom_call" | custom-call | flops 1610612736 | bytes 393216 | tf_op jit(solution)/shard_map/pallas_call | solution.py:247
  38.6 1.2 %copy.6 = f32[256]{0:T(256)} copy(f32[256]{0:T(256)} %shard_map.46) | data formatting | bytes 2048

commit v4 on v3

--- a/solution.py
+++ b/solution.py
@@ -24,7 +24,7 @@
     return out
 
 
-def kernel(groups, total, order, emb_hbm, group_hbm, cluster_hbm, order_hbm, out_ref, emb_ref, ids, fetched,
+def kernel(groups, total, perm, first_sends, emb_hbm, group_hbm, cluster_hbm, order_hbm, out_ref, emb_ref, ids, fetched,
            send, keys, msend, meta, kmeta, res, back, s1, r1, sm, rm, sy, ry, sc, rc, sd, rd, smx, rmx, sb, rb):
     points, width = emb_ref.shape
     cap = 2 * points // groups
@@ -35,7 +35,7 @@
     own = lax.axis_index("blk")
     across = {"blk": flip(own, 2)}
     beside = {"blk": flip(own, 1)}
-    partner = [None] + [{"dp": flip(me, k)} for k in range(1, groups)]
+    partner = [None] + [{"dp": flip(me, k)} for k in perm[1:]]
 
     fetches = [
         pltpu.make_async_copy(group_hbm, ids.at[0], fetched.at[0]),
@@ -59,7 +59,10 @@
         fetch.wait()
     group = ids[0]
     combined = ids[1] * total + ids[2] + 1
-    relative = jnp.bitwise_xor(group, me)
+    flipped = jnp.bitwise_xor(group, me)
+    relative = jnp.zeros_like(flipped)
+    for i, k in enumerate(perm):
+        relative = jnp.where(flipped == k, i, relative)
     member = lax.broadcasted_iota(jnp.int32, (groups, points), 0) == relative
     member_f = jnp.where(member, 1.0, 0.0)
     earlier = lax.broadcasted_iota(jnp.int32, (points, points), 0) < lax.broadcasted_iota(
@@ -96,42 +99,40 @@
 
     pl.semaphore_wait(barrier, groups + 1)
 
-    started = []
     meta_copies = [None] * groups
-    for k in order:
-        meta_copies[k] = remote(msend.at[k], meta.at[0, k], sm.at[k], rm.at[k], partner[k])
-        meta_copies[k].start()
+    for i in range(1, groups):
+        meta_copies[i] = remote(msend.at[i], meta.at[0, i], sm.at[i], rm.at[i], partner[i])
+        meta_copies[i].start()
 
     first = [None] * groups
     over_y = [None] * groups
     over_c = [None] * groups
     diag = [None] * groups
 
-    def forward(k):
-        over_y[k] = remote(keys.at[0, k], keys.at[2, k], sy.at[k], ry.at[k], across)
-        over_y[k].start()
-        over_c[k] = remote(keys.at[0, k], keys.at[1, k], sc.at[k], rc.at[k], beside)
-        over_c[k].start()
-
-    def onward(k):
-        over_y[k].wait_recv()
-        diag[k] = remote(keys.at[2, k], keys.at[3, k], sd.at[k], rd.at[k], beside)
-        diag[k].start()
-
+    def forward(i):
+        over_y[i] = remote(keys.at[0, i], keys.at[2, i], sy.at[i], ry.at[i], across)
+        over_y[i].start()
+        over_c[i] = remote(keys.at[0, i], keys.at[1, i], sc.at[i], rc.at[i], beside)
+        over_c[i].start()
+
+    def onward(i):
+        over_y[i].wait_recv()
+        diag[i] = remote(keys.at[2, i], keys.at[3, i], sd.at[i], rd.at[i], beside)
+        diag[i].start()
+
+    held_back = [i for i in range(1, groups) if i not in first_sends]
     slot_rows = lax.broadcasted_iota(jnp.int32, (cap, points), 0)
-    window = groups // 4
-    held_back = [k for k in order if k >= groups // 2][window:]
-    for k in [order[0], 0] + list(order[1:]):
-        place = jnp.where(slot_rows + k * cap == target, 1.0, 0.0).astype(jnp.bfloat16)
+    for i in first_sends + held_back:
+        place = jnp.where(slot_rows + i * cap == target, 1.0, 0.0).astype(jnp.bfloat16)
         rows = jnp.dot(place, unit, preferred_element_type=jnp.float32).astype(jnp.bfloat16)
-        if k == 0:
+        if i == 0:
             keys[0, 0] = rows
             forward(0)
         else:
-            send[k] = rows
-            first[k] = remote(send.at[k], keys.at[0, k], s1.at[k], r1.at[k], partner[k])
-            if k not in held_back:
-                first[k].start()
+            send[i] = rows
+            first[i] = remote(send.at[i], keys.at[0, i], s1.at[i], r1.at[i], partner[i])
+            if i not in held_back:
+                first[i].start()
 
     def key_tiles(r):
         lane_block = lax.broadcasted_iota(jnp.int32, (1, LANES), 1) // cap
@@ -144,64 +145,75 @@
             kmeta[r, t] = jnp.broadcast_to(row, (LANES, LANES)).T
         return rows
 
-    for k in order:
-        meta_copies[k].wait_recv()
+    for i in range(1, groups):
+        meta_copies[i].wait_recv()
     meta_y = remote(meta.at[0], meta.at[2], smx.at[0], rmx.at[0], across)
     meta_y.start()
     meta_c = remote(meta.at[0], meta.at[1], smx.at[1], rmx.at[1], beside)
     meta_c.start()
-    query = jnp.concatenate(key_tiles(0), axis=1)
-    floor = (query - 1) & (-total)
-
-    queue = [0]
-    for k in order:
-        first[k].wait_recv()
-        if k >= groups // 2 and held_back:
+    query = key_tiles(0)
+    floor = [(row - 1) & (-total) for row in query]
+    best = [jnp.full((8, LANES), -2.0, jnp.float32) for _ in range(tiles)]
+
+    def visit(r, t0, t1, q0, q1):
+        block = keys[r, t0 * per:t1 * per].reshape((t1 - t0) * LANES, width)
+        queries = keys[0, q0 * per:q1 * per].reshape((q1 - q0) * LANES, width)
+        scores = lax.dot_general(block, queries, NT, preferred_element_type=jnp.float32)
+        for t in range(t0, t1):
+            mine = kmeta[r, t]
+            for q in range(q0, q1):
+                part = scores[(t - t0) * LANES:(t - t0 + 1) * LANES, (q - q0) * LANES:(q - q0 + 1) * LANES]
+                part = jnp.where((mine < query[q]) & (mine > floor[q]), part, -2.0)
+                best[q] = jnp.maximum(best[q], jnp.max(part.reshape(LANES // 8, 8, LANES), axis=0))
+
+    def landed(r, t):
+        for i in range(t * per, (t + 1) * per):
+            if r == 1:
+                over_c[i].wait_recv()
+            if r == 3:
+                diag[i].wait_recv()
+
+    for i in range(1, groups):
+        first[i].wait_recv()
+        if perm[i] >= groups // 2 and held_back:
             first[held_back.pop(0)].start()
-        forward(k)
-        onward(queue.pop(0))
-        queue.append(k)
-        if k == order[1]:
+        forward(i)
+        onward(i - 1)
+        if i == 1:
+            meta_c.wait_recv()
+            key_tiles(1)
             meta_y.wait_recv()
             meta_d = remote(meta.at[2], meta.at[3], smx.at[2], rmx.at[2], beside)
             meta_d.start()
-    meta_c.wait_recv()
-    key_tiles(1)
-    key_tiles(2)
-    meta_d.wait_recv()
-    key_tiles(3)
-
-    queries = keys[0].reshape(slots, width)
-    half = groups // 2
-
-    def visit(best, r, h):
-        block = keys[r, h * half:(h + 1) * half].reshape(half * cap, width)
-        scores = lax.dot_general(block, queries, NT, preferred_element_type=jnp.float32)
-        for t in range(tiles // 2):
-            mine = kmeta[r, h * (tiles // 2) + t]
-            mine = jnp.concatenate([mine] * tiles, axis=1)
-            part = jnp.where((mine < query) & (mine > floor), scores[t * LANES:(t + 1) * LANES], -2.0)
-            best = jnp.maximum(best, jnp.max(part.reshape(LANES // 8, 8, slots), axis=0))
-        return best
-
-    best = jnp.full((8, slots), -2.0, jnp.float32)
-    best = visit(best, 0, 0)
-    onward(queue.pop(0))
-    for r in (0, 1, 2, 3):
-        for h in (0, 1):
-            if r == 0 and h == 0:
-                continue
-            if r == 1 or r == 3:
-                for k in range(h * half, (h + 1) * half):
-                    (over_c if r == 1 else diag)[k].wait_recv()
-            best = visit(best, r, h)
-    best = jnp.max(best, axis=0, keepdims=True)
+            key_tiles(2)
+            meta_d.wait_recv()
+            key_tiles(3)
+        if i % per == 0:
+            t = i // per - 1
+            if t:
+                for r in range(4):
+                    visit(r, 0, t, t, t + 1)
+            for r in (0, 2, 1, 3):
+                landed(r, t)
+                visit(r, t, t + 1, 0, t + 1)
+    last = tiles - 1
+    for r in range(4):
+        visit(r, 0, last, last, tiles)
+    visit(0, last, tiles, 0, tiles)
+    landed(1, last)
+    visit(1, last, tiles, 0, tiles)
+    onward(groups - 1)
+    visit(2, last, tiles, 0, tiles)
+    landed(3, last)
+    visit(3, last, tiles, 0, tiles)
+
+    best = jnp.concatenate([jnp.max(part, axis=0, keepdims=True) for part in best], axis=1)
     answer = jnp.broadcast_to(jnp.where(best > -1.5, best, -1.0), (8, slots))
     for t in range(tiles):
         res[t] = answer[:, t * LANES:(t + 1) * LANES]
     back[0] = res[0]
     replies = [None] * groups
-    for k in order:
+    for k in range(1, groups):
         replies[k] = remote(res.at[k // per], back.at[k], sb.at[k], rb.at[k], partner[k])
         replies[k].start()
 
@@ -231,7 +243,7 @@
         hit = jnp.where(slot_iota + t * LANES == target, column, -2.0)
         nearest = jnp.maximum(nearest, jnp.max(hit, axis=0, keepdims=True))
     out_ref[...] = nearest.reshape(points)
-    for k in order:
+    for k in range(1, groups):
         replies[k].wait_send()
 
 
@@ -242,10 +254,13 @@
     cap = 2 * points // groups
     slots = groups * cap
     near, far = list(range(1, groups // 2)), list(range(groups // 2, groups))
-    order = [k for pair in zip(near, far) for k in pair] + far[len(near):]
+    perm = [0, near[0]] + [k for pair in zip(near[1:], far) for k in pair] + far[len(near) - 1:]
+    held = far[groups // 4:]
+    first_sends = [k for k in [far[0], 0] + perm[1:] if k not in held]
+    first_sends = [perm.index(k) for k in dict.fromkeys(first_sends)]
     dma = pltpu.SemaphoreType.DMA
     out = pl.pallas_call(
-        functools.partial(kernel, groups, total, order),
+        functools.partial(kernel, groups, total, perm, first_sends),
         out_shape=jax.ShapeDtypeStruct((points,), jnp.float32),
         in_specs=[pl.BlockSpec(memory_space=pl.ANY)] * 4,
         out_specs=pl.BlockSpec(memory_space=pltpu.VMEM),

time: 40 us -> 40.3 us (level)
  no operation moved by 1% of the time
where the time goes in v4:
time: 40.3 us; the launch traced here: 40.1 us
  Pallas kernels  38.9 us (97%)
  local copies, waits for them, and re-layouts  1.24 us (3%)
    pallas_call x1, Pallas kernels, body(): pl.pallas_call(functools.partial(kernel, groups, total, perm, first_sends...  38.9 us
    unnamed x1, local copies, waits for them, and re-layouts  1.24 us

profile of v4, /device:TPU:0, one launch (start us, length us, event | category | flops | bytes accessed | tf_op | source)
XLA Modules:
  0.0 40.1 jit_solution(7499717166350919562)
XLA Ops:
  0.0 38.9 %shard_map.46 = f32[256]{0:T(256)} custom-call(bf16[256,768]{1,0:T(8,128)(2,1)} %emb_hbm.1, s32[1,256]{1,0:T(1,128)} %bitcast.3, s32[1,256]{1,0:T(1,128)} %bitcast.4, s32[1,256]{1,0:T(1,128)} %bitcast.5), custom_call_target="tpu_custom_call" | custom-call | flops 1610612736 | bytes 393216 | tf_op jit(solution)/shard_map/pallas_call | solution.py:262
  38.9 1.2 %copy.6 = f32[256]{0:T(256)} copy(f32[256]{0:T(256)} %shard_map.46) | data formatting | bytes 2048

commit v5 on v4

--- a/solution.py
+++ b/solution.py
@@ -175,16 +175,17 @@
 
     for i in range(1, groups):
         first[i].wait_recv()
-        if perm[i] >= groups // 2 and held_back:
+        if held_back:
             first[held_back.pop(0)].start()
         forward(i)
         onward(i - 1)
         if i == 1:
-            meta_c.wait_recv()
-            key_tiles(1)
             meta_y.wait_recv()
             meta_d = remote(meta.at[2], meta.at[3], smx.at[2], rmx.at[2], beside)
             meta_d.start()
+        if i == per:
+            meta_c.wait_recv()
+            key_tiles(1)
             key_tiles(2)
             meta_d.wait_recv()
             key_tiles(3)
@@ -254,10 +255,8 @@
     cap = 2 * points // groups
     slots = groups * cap
     near, far = list(range(1, groups // 2)), list(range(groups // 2, groups))
-    perm = [0, near[0]] + [k for pair in zip(near[1:], far) for k in pair] + far[len(near) - 1:]
-    held = far[groups // 4:]
-    first_sends = [k for k in [far[0], 0] + perm[1:] if k not in held]
-    first_sends = [perm.index(k) for k in dict.fromkeys(first_sends)]
+    perm = [0] + [k for pair in zip(near, far) for k in pair] + far[len(near):]
+    first_sends = [2, 0, 1]
     dma = pltpu.SemaphoreType.DMA
     out = pl.pallas_call(
         functools.partial(kernel, groups, total, perm, first_sends),

time: 40.3 us -> 41.3 us (1.025)
  Pallas kernels: 38.9 us -> 39.9 us
    pallas_call x1, Pallas kernels: 38.9 us -> 39.9 us  [body(): pl.pallas_call(functools.partial(kernel, groups, total, perm, first_sends...]
where the time goes in v5:
time: 41.3 us; the launch traced here: 41.2 us
  Pallas kernels  39.9 us (97%)
  local copies, waits for them, and re-layouts  1.24 us (3%)
    pallas_call x1, Pallas kernels, body(): pl.pallas_call(functools.partial(kernel, groups, total, perm, first_sends...  39.9 us
    unnamed x1, local copies, waits for them, and re-layouts  1.24 us

profile of v5, /device:TPU:0, one launch (start us, length us, event | category | flops | bytes accessed | tf_op | source)
XLA Modules:
  0.0 41.2 jit_solution(15764355441180701788)
XLA Ops:
  0.0 39.9 %shard_map.46 = f32[256]{0:T(256)} custom-call(bf16[256,768]{1,0:T(8,128)(2,1)} %emb_hbm.1, s32[1,256]{1,0:T(1,128)} %bitcast.3, s32[1,256]{1,0:T(1,128)} %bitcast.4, s32[1,256]{1,0:T(1,128)} %bitcast.5), custom_call_target="tpu_custom_call" | custom-call | flops 1610612736 | bytes 393216 | tf_op jit(solution)/shard_map/pallas_call | solution.py:261
  39.9 1.2 %copy.6 = f32[256]{0:T(256)} copy(f32[256]{0:T(256)} %shard_map.46) | data formatting | bytes 2048

commit v6 on v5

--- a/solution.py
+++ b/solution.py
@@ -76,6 +76,51 @@
     rank = jnp.sum(before * member_f, axis=0, keepdims=True).astype(jnp.int32)
     target = relative * cap + rank
 
+    fetches[3].wait()
+    values = emb_ref[...].astype(jnp.float32)
+    scale = lax.rsqrt(jnp.mean(values * values, axis=1, keepdims=True) + 1e-06)
+    unit = (values * scale * width ** (-0.5)).astype(jnp.bfloat16)
+
+    slot_rows = lax.broadcasted_iota(jnp.int32, (cap, points), 0)
+
+    def slotted(i):
+        place = jnp.where(slot_rows + i * cap == target, 1.0, 0.0).astype(jnp.bfloat16)
+        return jnp.dot(place, unit, preferred_element_type=jnp.float32).astype(jnp.bfloat16)
+
+    for i in first_sends:
+        if i == 0:
+            keys[0, 0] = slotted(0)
+        else:
+            send[i] = slotted(i)
+
+    pl.semaphore_wait(barrier, groups + 1)
+
+    first = [None] * groups
+    over_y = [None] * groups
+    over_c = [None] * groups
+    diag = [None] * groups
+
+    def forward(i):
+        over_y[i] = remote(keys.at[0, i], keys.at[2, i], sy.at[i], ry.at[i], across)
+        over_y[i].start()
+        over_c[i] = remote(keys.at[0, i], keys.at[1, i], sc.at[i], rc.at[i], beside)
+        over_c[i].start()
+
+    def onward(i):
+        over_y[i].wait_recv()
+        diag[i] = remote(keys.at[2, i], keys.at[3, i], sd.at[i], rd.at[i], beside)
+        diag[i].start()
+
+    def emit(i):
+        first[i] = remote(send.at[i], keys.at[0, i], s1.at[i], r1.at[i], partner[i])
+        first[i].start()
+
+    for i in first_sends:
+        if i == 0:
+            forward(0)
+        else:
+            emit(i)
+    held_back = [i for i in range(1, groups) if i not in first_sends]
     digits = jnp.concatenate(
         [combined & 127, (combined >> 7) & 127, combined >> 14, jnp.zeros((5, points), jnp.int32)], axis=0
     ).astype(jnp.float32).astype(jnp.bfloat16)
@@ -92,47 +137,13 @@
         else:
             msend[k] = row
 
-    fetches[3].wait()
-    values = emb_ref[...].astype(jnp.float32)
-    scale = lax.rsqrt(jnp.mean(values * values, axis=1, keepdims=True) + 1e-06)
-    unit = (values * scale * width ** (-0.5)).astype(jnp.bfloat16)
-
-    pl.semaphore_wait(barrier, groups + 1)
-
     meta_copies = [None] * groups
     for i in range(1, groups):
         meta_copies[i] = remote(msend.at[i], meta.at[0, i], sm.at[i], rm.at[i], partner[i])
         meta_copies[i].start()
 
-    first = [None] * groups
-    over_y = [None] * groups
-    over_c = [None] * groups
-    diag = [None] * groups
-
-    def forward(i):
-        over_y[i] = remote(keys.at[0, i], keys.at[2, i], sy.at[i], ry.at[i], across)
-        over_y[i].start()
-        over_c[i] = remote(keys.at[0, i], keys.at[1, i], sc.at[i], rc.at[i], beside)
-        over_c[i].start()
-
-    def onward(i):
-        over_y[i].wait_recv()
-        diag[i] = remote(keys.at[2, i], keys.at[3, i], sd.at[i], rd.at[i], beside)
-        diag[i].start()
-
-    held_back = [i for i in range(1, groups) if i not in first_sends]
-    slot_rows = lax.broadcasted_iota(jnp.int32, (cap, points), 0)
-    for i in first_sends + held_back:
-        place = jnp.where(slot_rows + i * cap == target, 1.0, 0.0).astype(jnp.bfloat16)
-        rows = jnp.dot(place, unit, preferred_element_type=jnp.float32).astype(jnp.bfloat16)
-        if i == 0:
-            keys[0, 0] = rows
-            forward(0)
-        else:
-            send[i] = rows
-            first[i] = remote(send.at[i], keys.at[0, i], s1.at[i], r1.at[i], partner[i])
-            if i not in held_back:
-                first[i].start()
+    for i in held_back:
+        send[i] = slotted(i)
 
     def key_tiles(r):
         lane_block = lax.broadcasted_iota(jnp.int32, (1, LANES), 1) // cap
@@ -151,8 +162,7 @@
     meta_y.start()
     meta_c = remote(meta.at[0], meta.at[1], smx.at[1], rmx.at[1], beside)
     meta_c.start()
-    query = key_tiles(0)
-    floor = [(row - 1) & (-total) for row in query]
+    ready, scored = False, 0
     best = [jnp.full((8, LANES), -2.0, jnp.float32) for _ in range(tiles)]
 
     def visit(r, t0, t1, q0, q1):
@@ -175,22 +185,27 @@
 
     for i in range(1, groups):
         first[i].wait_recv()
-        if held_back:
-            first[held_back.pop(0)].start()
+        if (i == 1 or perm[i] >= groups // 2) and held_back:
+            emit(held_back.pop(0))
         forward(i)
         onward(i - 1)
         if i == 1:
             meta_y.wait_recv()
             meta_d = remote(meta.at[2], meta.at[3], smx.at[2], rmx.at[2], beside)
             meta_d.start()
-        if i == per:
+        if held_back or i == groups - 1:
+            continue
+        if not ready:
             meta_c.wait_recv()
-            key_tiles(1)
-            key_tiles(2)
             meta_d.wait_recv()
-            key_tiles(3)
-        if i % per == 0:
-            t = i // per - 1
+            query = key_tiles(0)
+            floor = [(row - 1) & (-total) for row in query]
+            for r in (1, 2, 3):
+                key_tiles(r)
+            ready = True
+        while scored < i // per:
+            t = scored
+            scored += 1
             if t:
                 for r in range(4):
                     visit(r, 0, t, t, t + 1)
@@ -198,6 +213,7 @@
                 landed(r, t)
                 visit(r, t, t + 1, 0, t + 1)
     last = tiles - 1
+    assert ready and scored == last
     for r in range(4):
         visit(r, 0, last, last, tiles)
     visit(0, last, tiles, 0, tiles)
@@ -255,8 +271,9 @@
     cap = 2 * points // groups
     slots = groups * cap
     near, far = list(range(1, groups // 2)), list(range(groups // 2, groups))
-    perm = [0] + [k for pair in zip(near, far) for k in pair] + far[len(near):]
-    first_sends = [2, 0, 1]
+    perm = [0, near[0]] + [k for pair in zip(near[1:], far) for k in pair] + far[len(near) - 1:]
+    held = far[1:]
+    first_sends = [perm.index(k) for k in [far[0], 0] + near]
     dma = pltpu.SemaphoreType.DMA
     out = pl.pallas_call(
         functools.partial(kernel, groups, total, perm, first_sends),

time: 41.3 us -> 43.2 us (1.046)
  Pallas kernels: 39.9 us -> 41.7 us
    pallas_call x1, Pallas kernels: 39.9 us -> 41.7 us  [body(): pl.pallas_call(functools.partial(kernel, groups, total, perm, first_sends...]
where the time goes in v6:
time: 43.2 us; the launch traced here: 43 us
  Pallas kernels  41.7 us (97%)
  local copies, waits for them, and re-layouts  1.24 us (3%)
    pallas_call x1, Pallas kernels, body(): pl.pallas_call(functools.partial(kernel, groups, total, perm, first_sends...  41.7 us
    unnamed x1, local copies, waits for them, and re-layouts  1.24 us

profile of v6, /device:TPU:0, one launch (start us, length us, event | category | flops | bytes accessed | tf_op | source)
XLA Modules:
  0.0 43.0 jit_solution(3514386848425799599)
XLA Ops:
  0.0 41.7 %shard_map.46 = f32[256]{0:T(256)} custom-call(bf16[256,768]{1,0:T(8,128)(2,1)} %emb_hbm.1, s32[1,256]{1,0:T(1,128)} %bitcast.3, s32[1,256]{1,0:T(1,128)} %bitcast.4, s32[1,256]{1,0:T(1,128)} %bitcast.5), custom_call_target="tpu_custom_call" | custom-call | flops 1610612736 | bytes 393216 | tf_op jit(solution)/shard_map/pallas_call | solution.py:278
  41.8 1.2 %copy.6 = f32[256]{0:T(256)} copy(f32[256]{0:T(256)} %shard_map.46) | data formatting | bytes 2048

commit v7 on v6

--- a/solution.py
+++ b/solution.py
@@ -87,12 +87,6 @@
         place = jnp.where(slot_rows + i * cap == target, 1.0, 0.0).astype(jnp.bfloat16)
         return jnp.dot(place, unit, preferred_element_type=jnp.float32).astype(jnp.bfloat16)
 
-    for i in first_sends:
-        if i == 0:
-            keys[0, 0] = slotted(0)
-        else:
-            send[i] = slotted(i)
-
     pl.semaphore_wait(barrier, groups + 1)
 
     first = [None] * groups
@@ -117,10 +111,12 @@
 
     for i in first_sends:
         if i == 0:
+            keys[0, 0] = slotted(0)
             forward(0)
         else:
+            send[i] = slotted(i)
             emit(i)
-    held_back = [i for i in range(1, groups) if i not in first_sends]
+
     digits = jnp.concatenate(
         [combined & 127, (combined >> 7) & 127, combined >> 14, jnp.zeros((5, points), jnp.int32)], axis=0
     ).astype(jnp.float32).astype(jnp.bfloat16)
@@ -142,9 +138,6 @@
         meta_copies[i] = remote(msend.at[i], meta.at[0, i], sm.at[i], rm.at[i], partner[i])
         meta_copies[i].start()
 
-    for i in held_back:
-        send[i] = slotted(i)
-
     def key_tiles(r):
         lane_block = lax.broadcasted_iota(jnp.int32, (1, LANES), 1) // cap
         rows = []
@@ -162,7 +155,6 @@
     meta_y.start()
     meta_c = remote(meta.at[0], meta.at[1], smx.at[1], rmx.at[1], beside)
     meta_c.start()
-    ready, scored = False, 0
     best = [jnp.full((8, LANES), -2.0, jnp.float32) for _ in range(tiles)]
 
     def visit(r, t0, t1, q0, q1):
@@ -176,53 +168,47 @@
                 part = jnp.where((mine < query[q]) & (mine > floor[q]), part, -2.0)
                 best[q] = jnp.maximum(best[q], jnp.max(part.reshape(LANES // 8, 8, LANES), axis=0))
 
-    def landed(r, t):
-        for i in range(t * per, (t + 1) * per):
+    def landed(r, t0, t1):
+        for i in range(t0 * per, t1 * per):
             if r == 1:
                 over_c[i].wait_recv()
             if r == 3:
                 diag[i].wait_recv()
 
-    for i in range(1, groups):
+    middle = groups // 2
+    half = tiles // 2
+    for i in range(1, middle):
         first[i].wait_recv()
-        if (i == 1 or perm[i] >= groups // 2) and held_back:
-            emit(held_back.pop(0))
         forward(i)
         onward(i - 1)
         if i == 1:
             meta_y.wait_recv()
             meta_d = remote(meta.at[2], meta.at[3], smx.at[2], rmx.at[2], beside)
             meta_d.start()
-        if held_back or i == groups - 1:
-            continue
-        if not ready:
-            meta_c.wait_recv()
-            meta_d.wait_recv()
-            query = key_tiles(0)
-            floor = [(row - 1) & (-total) for row in query]
-            for r in (1, 2, 3):
-                key_tiles(r)
-            ready = True
-        while scored < i // per:
-            t = scored
-            scored += 1
-            if t:
-                for r in range(4):
-                    visit(r, 0, t, t, t + 1)
-            for r in (0, 2, 1, 3):
-                landed(r, t)
-                visit(r, t, t + 1, 0, t + 1)
-    last = tiles - 1
-    assert ready and scored == last
+    onward(middle - 1)
+    meta_c.wait_recv()
+    meta_d.wait_recv()
+    query = key_tiles(0)
+    floor = [(row - 1) & (-total) for row in query]
+    for r in (1, 2, 3):
+        key_tiles(r)
     for r in range(4):
-        visit(r, 0, last, last, tiles)
-    visit(0, last, tiles, 0, tiles)
-    landed(1, last)
-    visit(1, last, tiles, 0, tiles)
-    onward(groups - 1)
-    visit(2, last, tiles, 0, tiles)
-    landed(3, last)
-    visit(3, last, tiles, 0, tiles)
+        landed(r, 0, half)
+        visit(r, 0, half, 0, half)
+
+    for i in range(middle, groups):
+        first[i].wait_recv()
+        forward(i)
+    for r in range(4):
+        visit(r, 0, half, half, tiles)
+    visit(0, half, tiles, 0, tiles)
+    for i in range(middle, groups):
+        onward(i)
+    landed(1, half, tiles)
+    visit(1, half, tiles, 0, tiles)
+    visit(2, half, tiles, 0, tiles)
+    landed(3, half, tiles)
+    visit(3, half, tiles, 0, tiles)
 
     best = jnp.concatenate([jnp.max(part, axis=0, keepdims=True) for part in best], axis=1)
     answer = jnp.broadcast_to(jnp.where(best > -1.5, best, -1.0), (8, slots))
@@ -271,9 +257,8 @@
     cap = 2 * points // groups
     slots = groups * cap
     near, far = list(range(1, groups // 2)), list(range(groups // 2, groups))
-    perm = [0, near[0]] + [k for pair in zip(near[1:], far) for k in pair] + far[len(near) - 1:]
-    held = far[1:]
-    first_sends = [perm.index(k) for k in [far[0], 0] + near]
+    perm = [0] + near + far
+    first_sends = [near[0], 0] + [k for pair in zip(far, near[1:]) for k in pair] + far[len(near) - 1:]
     dma = pltpu.SemaphoreType.DMA
     out = pl.pallas_call(
         functools.partial(kernel, groups, total, perm, first_sends),

time: 43.2 us -> 55.6 us (1.29)
  Pallas kernels: 41.7 us -> 54.2 us
    pallas_call x1, Pallas kernels: 41.7 us -> 54.2 us  [body(): pl.pallas_call(functools.partial(kernel, groups, total, perm, first_sends...]
where the time goes in v7:
time: 55.6 us; the launch traced here: 55.5 us
  Pallas kernels  54.2 us (97%)
  local copies, waits for them, and re-layouts  1.24 us (2%)
    pallas_call x1, Pallas kernels, body(): pl.pallas_call(functools.partial(kernel, groups, total, perm, first_sends...  54.2 us
    unnamed x1, local copies, waits for them, and re-layouts  1.24 us

profile of v7, /device:TPU:0, one launch (start us, length us, event | category | flops | bytes accessed | tf_op | source)
XLA Modules:
  0.0 55.5 jit_solution(15358083577150684786)
XLA Ops:
  0.0 54.2 %shard_map.46 = f32[256]{0:T(256)} custom-call(bf16[256,768]{1,0:T(8,128)(2,1)} %emb_hbm.1, s32[1,256]{1,0:T(1,128)} %bitcast.3, s32[1,256]{1,0:T(1,128)} %bitcast.4, s32[1,256]{1,0:T(1,128)} %bitcast.5), custom_call_target="tpu_custom_call" | custom-call | flops 1610612736 | bytes 393216 | tf_op jit(solution)/shard_map/pallas_call | solution.py:263
  54.2 1.2 %copy.6 = f32[256]{0:T(256)} copy(f32[256]{0:T(256)} %shard_map.46) | data formatting | bytes 2048

commit v8 on v2

--- a/solution.py
+++ b/solution.py
@@ -25,7 +25,7 @@
 
 
 def kernel(groups, total, order, emb_hbm, group_hbm, cluster_hbm, order_hbm, out_ref, emb_ref, ids, fetched,
-           send, keys, msend, meta, kmeta, res, back, s1, r1, sm, rm, sy, ry, sc, rc, sd, rd, smx, rmx, sb, rb):
+           send, keys, msend, meta, kmeta, best, res, back, s1, r1, sm, rm, sy, ry, sc, rc, smx, rmx, sb, rb, s2, r2, s3):
     points, width = emb_ref.shape
     cap = 2 * points // groups
     slots = groups * cap
@@ -46,8 +46,12 @@
     for fetch in fetches:
         fetch.start()
 
+    lead = lax.rem(own, jnp.int32(2)) == 0
+    rows_of = [me] + [flip(me, k) for k in range(1, groups)]
+    far_y = [{"dp": row, "blk": flip(own, 2)} for row in rows_of]
+    far_c = [{"dp": row, "blk": flip(own, 1)} for row in rows_of]
     barrier = pltpu.get_barrier_semaphore()
-    for who in partner[1:] + [across, beside]:
+    for who in partner[1:] + far_y + far_c:
         pl.semaphore_signal(barrier, inc=1, device_id=who, device_id_type=MESH)
 
     def remote(src, dst, ssem, rsem, who):
@@ -94,7 +98,7 @@
     scale = lax.rsqrt(jnp.mean(values * values, axis=1, keepdims=True) + 1e-06)
     unit = (values * scale * width ** (-0.5)).astype(jnp.bfloat16)
 
-    pl.semaphore_wait(barrier, groups + 1)
+    pl.semaphore_wait(barrier, 3 * groups - 1)
 
     started = []
     meta_copies = [None] * groups
@@ -105,18 +109,12 @@
     first = [None] * groups
     over_y = [None] * groups
     over_c = [None] * groups
-    diag = [None] * groups
 
     def forward(k):
         over_y[k] = remote(keys.at[0, k], keys.at[2, k], sy.at[k], ry.at[k], across)
         over_y[k].start()
         over_c[k] = remote(keys.at[0, k], keys.at[1, k], sc.at[k], rc.at[k], beside)
-        over_c[k].start()
-
-    def onward(k):
-        over_y[k].wait_recv()
-        diag[k] = remote(keys.at[2, k], keys.at[3, k], sd.at[k], rd.at[k], beside)
-        diag[k].start()
+        pl.when(jnp.logical_not(lead))(over_c[k].start)
 
     slot_rows = lax.broadcasted_iota(jnp.int32, (cap, points), 0)
     for k in [order[0], 0] + list(order[1:]):
@@ -130,7 +128,7 @@
             first[k] = remote(send.at[k], keys.at[0, k], s1.at[k], r1.at[k], partner[k])
             first[k].start()
 
-    def key_tiles(r):
+    def key_rows(r):
         lane_block = lax.broadcasted_iota(jnp.int32, (1, LANES), 1) // cap
         rows = []
         for t in range(tiles):
@@ -138,8 +136,11 @@
             for j in range(1, per):
                 row = jnp.where(lane_block == j, meta[r, t * per + j][0:1, :], row)
             rows.append(row)
+        return rows
+
+    def key_tiles(r):
+        for t, row in enumerate(key_rows(r)):
             kmeta[r, t] = jnp.broadcast_to(row, (LANES, LANES)).T
-        return rows
 
     for k in order:
         meta_copies[k].wait_recv()
@@ -147,69 +148,85 @@
     meta_y.start()
     meta_c = remote(meta.at[0], meta.at[1], smx.at[1], rmx.at[1], beside)
     meta_c.start()
-    query = jnp.concatenate(key_tiles(0), axis=1)
-    floor = (query - 1) & (-total)
-
-    queue = [0]
+    key_tiles(0)
+    best[...] = jnp.full_like(best, -2.0)
+
     for k in order:
         first[k].wait_recv()
         forward(k)
-        onward(queue.pop(0))
-        queue.append(k)
-        if k == order[1]:
-            meta_y.wait_recv()
-            meta_d = remote(meta.at[2], meta.at[3], smx.at[2], rmx.at[2], beside)
-            meta_d.start()
+    meta_y.wait_recv()
+    key_tiles(2)
     meta_c.wait_recv()
     key_tiles(1)
-    key_tiles(2)
-    meta_d.wait_recv()
-    key_tiles(3)
-
-    queries = keys[0].reshape(slots, width)
-    half = groups // 2
-
-    def visit(best, r, h):
-        block = keys[r, h * half:(h + 1) * half].reshape(half * cap, width)
-        scores = lax.dot_general(block, queries, NT, preferred_element_type=jnp.float32)
-        for t in range(tiles // 2):
-            mine = kmeta[r, h * (tiles // 2) + t]
-            mine = jnp.concatenate([mine] * tiles, axis=1)
-            part = jnp.where((mine < query) & (mine > floor), scores[t * LANES:(t + 1) * LANES], -2.0)
-            best = jnp.maximum(best, jnp.max(part.reshape(LANES // 8, 8, slots), axis=0))
-        return best
-
-    best = jnp.full((8, slots), -2.0, jnp.float32)
-    best = visit(best, 0, 0)
-    onward(queue.pop(0))
-    for r in (0, 1, 2, 3):
-        for h in (0, 1):
-            if r == 0 and h == 0:
-                continue
-            if r == 1 or r == 3:
-                for k in range(h * half, (h + 1) * half):
-                    (over_c if r == 1 else diag)[k].wait_recv()
-            best = visit(best, r, h)
-    best = jnp.max(best, axis=0, keepdims=True)
-    answer = jnp.broadcast_to(jnp.where(best > -1.5, best, -1.0), (8, slots))
-    for t in range(tiles):
-        res[t] = answer[:, t * LANES:(t + 1) * LANES]
-    back[0] = res[0]
+
+    half = tiles // 2
+
+    def visit(q, r):
+        queries = keys[q].reshape(slots, width)
+        query = jnp.concatenate(key_rows(q), axis=1)
+        floor = (query - 1) & (-total)
+        found = best[q]
+        for h in range(2):
+            block = keys[r, h * (groups // 2):(h + 1) * (groups // 2)].reshape(slots // 2, width)
+            scores = lax.dot_general(block, queries, NT, preferred_element_type=jnp.float32)
+            for t in range(half):
+                mine = jnp.concatenate([kmeta[r, h * half + t]] * tiles, axis=1)
+                part = jnp.where((mine < query) & (mine > floor), scores[t * LANES:(t + 1) * LANES], -2.0)
+                found = jnp.maximum(found, jnp.max(part.reshape(LANES // 8, 8, slots), axis=0))
+        best[q] = found
+
+    def answer(q):
+        found = jnp.max(best[q], axis=0, keepdims=True)
+        found = jnp.broadcast_to(found, (8, slots))
+        for t in range(tiles):
+            res[q, t] = found[:, t * LANES:(t + 1) * LANES]
+
+    visit(0, 0)
+
+    @pl.when(lead)
+    def _():
+        for k in range(groups):
+            over_c[k].wait_recv()
+        visit(1, 0)
+        visit(0, 1)
+
+    for k in range(groups):
+        over_y[k].wait_recv()
+
+    extra_y = [remote(res.at[2, k // per], back.at[1, k], s2.at[k], r2.at[k], far_y[k]) for k in range(groups)]
+    extra_c = [remote(res.at[1, k // per], back.at[1, k], s3.at[k], r2.at[k], far_c[k]) for k in range(groups)]
+
+    @pl.when(lead)
+    def _():
+        visit(2, 1)
+        answer(2)
+        for copy in extra_y:
+            copy.start()
+        visit(1, 2)
+        answer(1)
+        for copy in extra_c:
+            copy.start()
+
+    visit(0, 2)
+    answer(0)
+    back[0, 0] = res[0, 0]
     replies = [None] * groups
     for k in order:
-        replies[k] = remote(res.at[k // per], back.at[k], sb.at[k], rb.at[k], partner[k])
+        replies[k] = remote(res.at[0, k // per], back.at[0, k], sb.at[k], rb.at[k], partner[k])
         replies[k].start()
 
     for k in range(groups):
         over_y[k].wait_send()
-        over_c[k].wait_send()
-        diag[k].wait_send()
         if k:
             first[k].wait_send()
             meta_copies[k].wait_send()
     meta_y.wait_send()
     meta_c.wait_send()
-    meta_d.wait_send()
+
+    @pl.when(jnp.logical_not(lead))
+    def _():
+        for k in range(groups):
+            over_c[k].wait_send()
 
     lane_block = lax.broadcasted_iota(jnp.int32, (1, LANES), 1) // cap
     nearest = jnp.full((1, points), -2.0, jnp.float32)
@@ -218,16 +235,24 @@
         for j in range(per):
             if t * per + j:
                 replies[t * per + j].wait_recv()
-        row = back[t * per][0:1, :]
+            extra_y[t * per + j].wait_recv()
+        row = jnp.maximum(back[0, t * per], back[1, t * per])[0:1, :]
         for j in range(1, per):
-            row = jnp.where(lane_block == j, back[t * per + j][0:1, :], row)
+            pair = jnp.maximum(back[0, t * per + j], back[1, t * per + j])
+            row = jnp.where(lane_block == j, pair[0:1, :], row)
         column = jnp.broadcast_to(row, (LANES, LANES)).T
         column = jnp.concatenate([column] * (points // LANES), axis=1)
         hit = jnp.where(slot_iota + t * LANES == target, column, -2.0)
         nearest = jnp.maximum(nearest, jnp.max(hit, axis=0, keepdims=True))
-    out_ref[...] = nearest
+    out_ref[...] = jnp.where(nearest > -1.5, nearest, -1.0).reshape(points)
     for k in order:
         replies[k].wait_send()
+
+    @pl.when(lead)
+    def _():
+        for k in range(groups):
+            extra_y[k].wait_send()
+            extra_c[k].wait_send()
 
 
 def body(total, embeddings, point_group, point_cluster, point_order):
@@ -241,7 +266,7 @@
     dma = pltpu.SemaphoreType.DMA
     out = pl.pallas_call(
         functools.partial(kernel, groups, total, order),
-        out_shape=jax.ShapeDtypeStruct((1, points), jnp.float32),
+        out_shape=jax.ShapeDtypeStruct((points,), jnp.float32),
         in_specs=[pl.BlockSpec(memory_space=pl.ANY)] * 4,
         out_specs=pl.BlockSpec(memory_space=pltpu.VMEM),
         scratch_shapes=[
@@ -249,16 +274,17 @@
             pltpu.VMEM((3, 1, points), jnp.int32),
             dma((4,)),
             pltpu.VMEM((groups, cap, width), jnp.bfloat16),
-            pltpu.VMEM((blocks, groups, cap, width), jnp.bfloat16),
+            pltpu.VMEM((3, groups, cap, width), jnp.bfloat16),
             pltpu.VMEM((groups, 8, LANES), jnp.int32),
-            pltpu.VMEM((blocks, groups, 8, LANES), jnp.int32),
-            pltpu.VMEM((blocks, slots // LANES, LANES, LANES), jnp.int32),
-            pltpu.VMEM((slots // LANES, 8, LANES), jnp.float32),
-            pltpu.VMEM((groups, 8, LANES), jnp.float32),
+            pltpu.VMEM((3, groups, 8, LANES), jnp.int32),
+            pltpu.VMEM((3, slots // LANES, LANES, LANES), jnp.int32),
+            pltpu.VMEM((3, 8, slots), jnp.float32),
+            pltpu.VMEM((3, slots // LANES, 8, LANES), jnp.float32),
+            pltpu.VMEM((2, groups, 8, LANES), jnp.float32),
         ]
-        + [dma((groups,))] * 10
-        + [dma((3,))] * 2
-        + [dma((groups,))] * 2,
+        + [dma((groups,))] * 8
+        + [dma((2,))] * 2
+        + [dma((groups,))] * 5,
         compiler_params=pltpu.CompilerParams(
             collective_id=0, has_side_effects=True, vmem_limit_bytes=64 * 1024 * 1024 - 65536
         ),
@@ -266,7 +292,7 @@
             flops=2 * slots * slots * blocks * width, bytes_accessed=points * width * 2, transcendentals=points
         ),
     )(embeddings, point_group.reshape(1, points), point_cluster.reshape(1, points), point_order.reshape(1, points))
-    return out.reshape(points)
+    return out
 
 
 def solution(mesh):

time: 40.2 us -> 39.3 us (0.978)
  Pallas kernels: 38.9 us -> 37.8 us
    pallas_call x1, Pallas kernels: 38.9 us -> 37.8 us  [body(): pl.pallas_call(functools.partial(kernel, groups, total, order), out_shape...]
    unnamed x3 -> x1, local copies, waits for them, and re-layouts: 1.22 us -> 1.24 us
where the time goes in v8:
time: 39.3 us; the launch traced here: 39.1 us
  Pallas kernels  37.8 us (96%)
  local copies, waits for them, and re-layouts  1.24 us (3%)
    pallas_call x1, Pallas kernels, body(): pl.pallas_call(functools.partial(kernel, groups, total, order), out_shape...  37.8 us
    unnamed x1, local copies, waits for them, and re-layouts  1.24 us

profile of v8, /device:TPU:0, one launch (start us, length us, event | category | flops | bytes accessed | tf_op | source)
XLA Modules:
  0.0 39.1 jit_solution(8012343377897788221)
XLA Ops:
  0.0 37.8 %shard_map.46 = f32[256]{0:T(256)} custom-call(bf16[256,768]{1,0:T(8,128)(2,1)} %emb_hbm.1, s32[1,256]{1,0:T(1,128)} %bitcast.3, s32[1,256]{1,0:T(1,128)} %bitcast.4, s32[1,256]{1,0:T(1,128)} %bitcast.5), custom_call_target="tpu_custom_call" | custom-call | flops 1610612736 | bytes 393216 | tf_op jit(solution)/shard_map/pallas_call | solution.py:267
  37.8 1.2 %copy.6 = f32[256]{0:T(256)} copy(f32[256]{0:T(256)} %shard_map.46) | data formatting | bytes 2048

commit v9 on v8

--- a/solution.py
+++ b/solution.py
@@ -151,29 +151,24 @@
     key_tiles(0)
     best[...] = jnp.full_like(best, -2.0)
 
-    for k in order:
-        first[k].wait_recv()
-        forward(k)
-    meta_y.wait_recv()
-    key_tiles(2)
-    meta_c.wait_recv()
-    key_tiles(1)
-
-    half = tiles // 2
-
-    def visit(q, r):
-        queries = keys[q].reshape(slots, width)
-        query = jnp.concatenate(key_rows(q), axis=1)
+    middle, half = groups // 2, tiles // 2
+    both, near, far = (0, tiles), (0, half), (half, tiles)
+
+    def visit(q, r, q_span, r_span):
+        (q0, q1), (r0, r1) = q_span, r_span
+        wide = (q1 - q0) * LANES
+        queries = keys[q, q0 * per:q1 * per].reshape(wide, width)
+        query = jnp.concatenate(key_rows(q)[q0:q1], axis=1)
         floor = (query - 1) & (-total)
-        found = best[q]
-        for h in range(2):
-            block = keys[r, h * (groups // 2):(h + 1) * (groups // 2)].reshape(slots // 2, width)
+        found = best[q, :, q0 * LANES:q1 * LANES]
+        for t0 in range(r0, r1, half):
+            block = keys[r, t0 * per:(t0 + half) * per].reshape(half * LANES, width)
             scores = lax.dot_general(block, queries, NT, preferred_element_type=jnp.float32)
             for t in range(half):
-                mine = jnp.concatenate([kmeta[r, h * half + t]] * tiles, axis=1)
+                mine = jnp.concatenate([kmeta[r, t0 + t]] * (q1 - q0), axis=1)
                 part = jnp.where((mine < query) & (mine > floor), scores[t * LANES:(t + 1) * LANES], -2.0)
-                found = jnp.maximum(found, jnp.max(part.reshape(LANES // 8, 8, slots), axis=0))
-        best[q] = found
+                found = jnp.maximum(found, jnp.max(part.reshape(LANES // 8, 8, wide), axis=0))
+        best[q, :, q0 * LANES:q1 * LANES] = found
 
     def answer(q):
         found = jnp.max(best[q], axis=0, keepdims=True)
@@ -181,16 +176,41 @@
         for t in range(tiles):
             res[q, t] = found[:, t * LANES:(t + 1) * LANES]
 
-    visit(0, 0)
+    for k in order:
+        first[k].wait_recv()
+        forward(k)
+        if k == middle - 1:
+            meta_y.wait_recv()
+            key_tiles(2)
+            meta_c.wait_recv()
+            key_tiles(1)
+            visit(0, 0, near, near)
+    visit(0, 0, far, near)
+    visit(0, 0, both, far)
 
     @pl.when(lead)
     def _():
-        for k in range(groups):
+        for k in range(middle):
             over_c[k].wait_recv()
-        visit(1, 0)
-        visit(0, 1)
-
-    for k in range(groups):
+        visit(1, 0, near, both)
+        visit(0, 1, both, near)
+
+    for k in range(middle):
+        over_y[k].wait_recv()
+    visit(0, 2, both, near)
+
+    @pl.when(lead)
+    def _():
+        visit(2, 1, near, near)
+        visit(1, 2, near, near)
+        for k in range(middle, groups):
+            over_c[k].wait_recv()
+        visit(1, 0, far, both)
+        visit(0, 1, both, far)
+        visit(2, 1, near, far)
+        visit(1, 2, far, near)
+
+    for k in range(middle, groups):
         over_y[k].wait_recv()
 
     extra_y = [remote(res.at[2, k // per], back.at[1, k], s2.at[k], r2.at[k], far_y[k]) for k in range(groups)]
@@ -198,16 +218,16 @@
 
     @pl.when(lead)
     def _():
-        visit(2, 1)
+        visit(2, 1, far, both)
         answer(2)
         for copy in extra_y:
             copy.start()
-        visit(1, 2)
+        visit(1, 2, both, far)
         answer(1)
         for copy in extra_c:
             copy.start()
 
-    visit(0, 2)
+    visit(0, 2, both, far)
     answer(0)
     back[0, 0] = res[0, 0]
     replies = [None] * groups

time: 39.3 us -> 38.5 us (0.980)
  Pallas kernels: 37.8 us -> 37.1 us
    pallas_call x1, Pallas kernels: 37.8 us -> 37.1 us  [body(): pl.pallas_call(functools.partial(kernel, groups, total, order), out_shape...]
where the time goes in v9:
time: 38.5 us; the launch traced here: 38.3 us
  Pallas kernels  37.1 us (96%)
  local copies, waits for them, and re-layouts  1.24 us (3%)
    pallas_call x1, Pallas kernels, body(): pl.pallas_call(functools.partial(kernel, groups, total, order), out_shape...  37.1 us
    unnamed x1, local copies, waits for them, and re-layouts  1.24 us

profile of v9, /device:TPU:0, one launch (start us, length us, event | category | flops | bytes accessed | tf_op | source)
XLA Modules:
  0.0 38.3 jit_solution(1116235773700757053)
XLA Ops:
  0.0 37.1 %shard_map.46 = f32[256]{0:T(256)} custom-call(bf16[256,768]{1,0:T(8,128)(2,1)} %emb_hbm.1, s32[1,256]{1,0:T(1,128)} %bitcast.3, s32[1,256]{1,0:T(1,128)} %bitcast.4, s32[1,256]{1,0:T(1,128)} %bitcast.5), custom_call_target="tpu_custom_call" | custom-call | flops 1610612736 | bytes 393216 | tf_op jit(solution)/shard_map/pallas_call | solution.py:287
  37.1 1.2 %copy.6 = f32[256]{0:T(256)} copy(f32[256]{0:T(256)} %shard_map.46) | data formatting | bytes 2048

commit v10 on v9

--- a/solution.py
+++ b/solution.py
@@ -80,18 +80,15 @@
     digits = jnp.concatenate(
         [combined & 127, (combined >> 7) & 127, combined >> 14, jnp.zeros((5, points), jnp.int32)], axis=0
     ).astype(jnp.float32).astype(jnp.bfloat16)
-    lane_slot = lax.broadcasted_iota(jnp.int32, (LANES, points), 0) & (cap - 1)
-    local_target = target & (cap - 1)
-    same_rank = lane_slot == local_target
-    for k in range(groups):
-        pick = jnp.where(same_rank & (relative == k), 1.0, 0.0).astype(jnp.bfloat16)
-        got = lax.dot_general(digits, pick, NT, preferred_element_type=jnp.float32)
-        row = got[0:1, :] + 128.0 * got[1:2, :] + 16384.0 * got[2:3, :]
-        row = jnp.broadcast_to(row.astype(jnp.int32), (8, LANES))
-        if k == 0:
-            meta[0, 0] = row
-        else:
-            msend[k] = row
+    lane_row = lax.broadcasted_iota(jnp.int32, (groups * LANES, points), 0)
+    lane_slot = (lane_row // LANES) * cap + (lane_row & (cap - 1))
+    pick = jnp.where(lane_slot == target, 1.0, 0.0).astype(jnp.bfloat16)
+    got = lax.dot_general(digits, pick, NT, preferred_element_type=jnp.float32)
+    row = got[0:1, :] + 128.0 * got[1:2, :] + 16384.0 * got[2:3, :]
+    row = jnp.broadcast_to(row.astype(jnp.int32), (8, groups * LANES))
+    meta[0, 0] = row[:, :LANES]
+    for k in range(1, groups):
+        msend[k] = row[:, k * LANES:(k + 1) * LANES]
 
     fetches[3].wait()
     values = emb_ref[...].astype(jnp.float32)
@@ -117,16 +114,32 @@
         pl.when(jnp.logical_not(lead))(over_c[k].start)
 
     slot_rows = lax.broadcasted_iota(jnp.int32, (cap, points), 0)
-    for k in [order[0], 0] + list(order[1:]):
+    plans = [[order[0], 0] + list(order[1:]), [order[1], order[0], 0, order[3], order[2]] + list(order[4:])]
+    ready = []
+    for k in [order[0], order[1], 0, order[3], order[2]] + list(order[4:]):
         place = jnp.where(slot_rows + k * cap == target, 1.0, 0.0).astype(jnp.bfloat16)
         rows = jnp.dot(place, unit, preferred_element_type=jnp.float32).astype(jnp.bfloat16)
         if k == 0:
             keys[0, 0] = rows
-            forward(0)
         else:
             send[k] = rows
             first[k] = remote(send.at[k], keys.at[0, k], s1.at[k], r1.at[k], partner[k])
-            first[k].start()
+        ready.append(k)
+        if len(ready) == 1:
+            continue
+        for plan, mine in zip(plans, (lead, jnp.logical_not(lead))):
+            go = []
+            while plan and plan[0] in ready:
+                go.append(plan.pop(0))
+
+            @pl.when(mine)
+            def _(go=tuple(go)):
+                for j in go:
+                    if j:
+                        first[j].start()
+
+        if k == 0:
+            forward(0)
 
     def key_rows(r):
         lane_block = lax.broadcasted_iota(jnp.int32, (1, LANES), 1) // cap

time: 38.5 us -> 39.1 us (1.016)
  Pallas kernels: 37.1 us -> 37.7 us
    pallas_call x1, Pallas kernels: 37.1 us -> 37.7 us  [body(): pl.pallas_call(functools.partial(kernel, groups, total, order), out_shape...]
where the time goes in v10:
time: 39.1 us; the launch traced here: 38.9 us
  Pallas kernels  37.7 us (96%)
  local copies, waits for them, and re-layouts  1.24 us (3%)
    pallas_call x1, Pallas kernels, body(): pl.pallas_call(functools.partial(kernel, groups, total, order), out_shape...  37.7 us
    unnamed x1, local copies, waits for them, and re-layouts  1.24 us

profile of v10, /device:TPU:0, one launch (start us, length us, event | category | flops | bytes accessed | tf_op | source)
XLA Modules:
  0.0 38.9 jit_solution(4175150421090966111)
XLA Ops:
  0.0 37.7 %shard_map.46 = f32[256]{0:T(256)} custom-call(bf16[256,768]{1,0:T(8,128)(2,1)} %emb_hbm.1, s32[1,256]{1,0:T(1,128)} %bitcast.3, s32[1,256]{1,0:T(1,128)} %bitcast.4, s32[1,256]{1,0:T(1,128)} %bitcast.5), custom_call_target="tpu_custom_call" | custom-call | flops 1610612736 | bytes 393216 | tf_op jit(solution)/shard_map/pallas_call | solution.py:300
  37.7 1.2 %copy.6 = f32[256]{0:T(256)} copy(f32[256]{0:T(256)} %shard_map.46) | data formatting | bytes 2048

commit v11 on v10

--- a/solution.py
+++ b/solution.py
@@ -114,32 +114,16 @@
         pl.when(jnp.logical_not(lead))(over_c[k].start)
 
     slot_rows = lax.broadcasted_iota(jnp.int32, (cap, points), 0)
-    plans = [[order[0], 0] + list(order[1:]), [order[1], order[0], 0, order[3], order[2]] + list(order[4:])]
-    ready = []
-    for k in [order[0], order[1], 0, order[3], order[2]] + list(order[4:]):
+    for k in [order[0], 0] + list(order[1:]):
         place = jnp.where(slot_rows + k * cap == target, 1.0, 0.0).astype(jnp.bfloat16)
         rows = jnp.dot(place, unit, preferred_element_type=jnp.float32).astype(jnp.bfloat16)
         if k == 0:
             keys[0, 0] = rows
+            forward(0)
         else:
             send[k] = rows
             first[k] = remote(send.at[k], keys.at[0, k], s1.at[k], r1.at[k], partner[k])
-        ready.append(k)
-        if len(ready) == 1:
-            continue
-        for plan, mine in zip(plans, (lead, jnp.logical_not(lead))):
-            go = []
-            while plan and plan[0] in ready:
-                go.append(plan.pop(0))
-
-            @pl.when(mine)
-            def _(go=tuple(go)):
-                for j in go:
-                    if j:
-                        first[j].start()
-
-        if k == 0:
-            forward(0)
+            first[k].start()
 
     def key_rows(r):
         lane_block = lax.broadcasted_iota(jnp.int32, (1, LANES), 1) // cap

time: 39.1 us -> 38.5 us (0.985)
  Pallas kernels: 37.7 us -> 37.1 us
    pallas_call x1, Pallas kernels: 37.7 us -> 37.1 us  [body(): pl.pallas_call(functools.partial(kernel, groups, total, order), out_shape...]
where the time goes in v11:
time: 38.5 us; the launch traced here: 38.3 us
  Pallas kernels  37.1 us (96%)
  local copies, waits for them, and re-layouts  1.24 us (3%)
    pallas_call x1, Pallas kernels, body(): pl.pallas_call(functools.partial(kernel, groups, total, order), out_shape...  37.1 us
    unnamed x1, local copies, waits for them, and re-layouts  1.24 us

profile of v11, /device:TPU:0, one launch (start us, length us, event | category | flops | bytes accessed | tf_op | source)
XLA Modules:
  0.0 38.3 jit_solution(16375638841058349597)
XLA Ops:
  0.0 37.1 %shard_map.46 = f32[256]{0:T(256)} custom-call(bf16[256,768]{1,0:T(8,128)(2,1)} %emb_hbm.1, s32[1,256]{1,0:T(1,128)} %bitcast.3, s32[1,256]{1,0:T(1,128)} %bitcast.4, s32[1,256]{1,0:T(1,128)} %bitcast.5), custom_call_target="tpu_custom_call" | custom-call | flops 1610612736 | bytes 393216 | tf_op jit(solution)/shard_map/pallas_call | solution.py:284
  37.1 1.2 %copy.6 = f32[256]{0:T(256)} copy(f32[256]{0:T(256)} %shard_map.46) | data formatting | bytes 2048
